TPU v7x, 128 devices: a whole 4x4x4 slice. The times are simulated.
128 devices in a mesh: ops: 4 (over z), sec: 32 (over y, x, core).
Axes of the slice: x: 4, y: 4, z: 4, core: 2. Of those that a mesh axis runs over, the one named last changes fastest.
Arguments:
- psi_blocks: bfloat16 [32, 16, 512, 512], P('sec'), may hold values from -6 to 6
- left_env: bfloat16 [4, 32, 512, 512], P('ops', 'sec'), may hold values from -0.25 to 0.25
- right_env: bfloat16 [4, 32, 512, 512], P('ops', 'sec'), may hold values from -0.25 to 0.25
- shifts: int32 [16], replicated, may hold values from 0 to 31, as said below
- sector_dims: int32 [32], replicated, may hold values from 64 to 512, as said below
Outputs:
- sigma_blocks: bfloat16 [32, 16, 512, 512], P('sec', 'ops')
Inputs may be any that keep to these rules, and one draw needn't show every extreme that they name: `shifts`: the values are distinct; 0, 1, 16 and 31 are among them. `sector_dims`: one sector has exactly 512 live states.
All inputs are finite; a program needn't handle non-finite values.
Results may differ from a plain program's by a relative error of at most 0.013.
Values may be sent and summed in bfloat16 or wider, within the bound.
A program may use at most 128 MiB of HBM per device.

v0:
```python
import jax
import jax.numpy as jnp
from jax import lax
from jax.sharding import PartitionSpec as P


def relayout_blocks(halfway, target, anchor, sectors):
    outgoing = jnp.zeros((sectors,) + halfway.shape[1:], jnp.bfloat16).at[target].set(halfway)
    arrived = lax.all_to_all(outgoing, "sec", split_axis=0, concat_axis=0, tiled=True)
    return arrived[anchor]


def body(psi_blocks, left_env, right_env, shifts, sector_dims):
    sectors = lax.axis_size("sec")
    own_index = lax.axis_index("sec")
    group_index = lax.axis_index("ops")
    group_count = lax.axis_size("ops")
    partners = psi_blocks.shape[1]
    block_width = psi_blocks.shape[2]
    quarter = partners // group_count
    positions = jnp.arange(block_width, dtype=jnp.int32)
    target = jnp.mod(own_index + shifts, sectors)
    anchor = jnp.mod(own_index - shifts, sectors)
    left_terms = left_env[:, 0]
    right_terms = right_env[:, 0]
    own_rows = positions < sector_dims[own_index]
    target_cols = positions[None, :] < sector_dims[target][:, None]
    blocks = jnp.where(
        own_rows[None, :, None] & target_cols[:, None, :],
        psi_blocks[0],
        jnp.zeros((), jnp.bfloat16),
    )
    halfway = jnp.einsum(
        "tij,pjk->ptik", left_terms, blocks, preferred_element_type=jnp.float32
    ).astype(jnp.bfloat16)
    own_anchor = lax.dynamic_slice_in_dim(anchor, group_index * quarter, quarter)
    row_mask = positions[None, :] < sector_dims[own_anchor][:, None]
    final_mask = row_mask[:, :, None] & own_rows[None, None, :]
    incoming = relayout_blocks(halfway, target, anchor, sectors)
    partial_value = jnp.einsum(
        "ptik,tkl->pil", incoming, right_terms, preferred_element_type=jnp.float32
    )
    partial_value = lax.optimization_barrier(partial_value.astype(jnp.bfloat16)).astype(jnp.float32)
    summed = lax.psum_scatter(
        partial_value.astype(jnp.bfloat16), "ops", scatter_dimension=0, tiled=True
    ).astype(jnp.float32)
    finished = jnp.where(final_mask, summed, jnp.zeros((), summed.dtype))
    return finished.astype(jnp.bfloat16)[None]


def solution(mesh):
    in_specs = (
        P("sec", None, None, None),
        P("ops", "sec", None, None),
        P("ops", "sec", None, None),
        P(),
        P(),
    )
    out_specs = P("sec", "ops", None, None)
    return jax.shard_map(body, mesh=mesh, in_specs=in_specs, out_specs=out_specs, check_vma=False)
```

profile of v0, /device:TPU:1, one launch (start us, length us, event | category | flops | bytes accessed | tf_op | source)
XLA Modules:
  0.0 393.7 jit_solution(18211650509624811733)
XLA Ops:
  6.5 0.0 copy-start
  6.5 1.3 dynamic_slice.7
  7.8 0.6 iota_compare_fusion.2
  8.5 0.7 compare_select_fusion
  9.2 1.3 gather_fusion.1
  10.5 0.1 iota_compare_fusion
  10.6 0.0 copy-done
  10.6 12.7 %convert_bitcast_fusion = bf16[16,512,512]{1,2,0:T(8,128)(2,1)} fusion(bf16[1,16,512,512]{3,2,1,0:T(8,128)(2,1)} %param.5, pred[16,512]{1,0:T(8,128)(4,1)S(1)} %iota_compare_fusion, pred[512]{0:T(512)(128)(4,1)S(1)} %iota_compare_fusion.2, bf16[1,1,512,512]{3,2,1,0:T(8,128)(2,1)S(1)} %copy-done), kind=kOutput, calls=%fused_computation.7 | convolution fusion | flops 4307550208 | bytes 17310208 | tf_op jit(solution)/shard_map/tij,pjk->ptik/dot_general | solution.py:33
  23.3 12.3 %copy.11 = bf16[16,512,512]{2,1,0:T(8,128)(2,1)} copy(bf16[16,512,512]{1,2,0:T(8,128)(2,1)} %convert_bitcast_fusion) | data formatting | bytes 16777216 | tf_op jit(solution)/shard_map/convert_element_type | solution.py:35
  35.6 5.9 %broadcast.66 = bf16[32,512,512]{2,1,0:T(8,128)(2,1)} broadcast(bf16[]{:T(256)} %constant.41.clone.1), dimensions={} | broadcast | bytes 16777218 | tf_op jit(solution)/shard_map/broadcast_in_dim | solution.py:8
  41.5 21.4 %scatter_fusion = bf16[32,512,512]{2,1,0:T(8,128)(2,1)} fusion(bf16[32,512,512]{2,1,0:T(8,128)(2,1)} %broadcast.66, s32[16]{0:T(128)S(1)} %get-tuple-element.7, bf16[16,512,512]{2,1,0:T(8,128)(2,1)} %copy.11), kind=kCustom, calls=%fused_computation.3 | custom fusion | bytes 25165888 | tf_op jit(solution)/shard_map/scatter | solution.py:8
  62.9 8.5 %all-to-all-start = ((bf16[32,1,512,512]{3,2,1,0:T(8,128)(2,1)}), bf16[32,1,512,512]{3,2,1,0:T(8,128)(2,1)}, u32[]{:S(2)}, u32[]{:S(2)}) async-start(bf16[32,1,512,512]{3,2,1,0:T(8,128)(2,1)} %bitcast.29), calls=%async_computation | async-start | bytes 33554432 | tf_op jit(solution)/shard_map/all_to_all | solution.py:9
  71.4 0.0 reduce-scatter.2.cloned.1.call-start
  71.5 201.9 %all-to-all-done = bf16[32,1,512,512]{3,2,1,0:T(8,128)(2,1)} async-done(((bf16[32,1,512,512]{3,2,1,0:T(8,128)(2,1)}), bf16[32,1,512,512]{3,2,1,0:T(8,128)(2,1)}, u32[]{:S(2)}, u32[]{:S(2)}) %all-to-all-start) | async-done | bytes 16777248 | tf_op jit(solution)/shard_map/all_to_all | solution.py:9
  273.4 10.6 %gather_fusion.2 = bf16[16,512,512]{2,1,0:T(8,128)(2,1)} fusion(bf16[32,512,512]{2,1,0:T(8,128)(2,1)} %bitcast.9, s32[1024]{0:T(1024)S(1)} %pad_clamp_fusion), kind=kCustom, calls=%fused_computation.2 | custom fusion | bytes 16777280 | tf_op jit(solution)/shard_map/gather | solution.py:10
  284.0 0.0 copy-done.3
  284.0 10.2 %convolution_convert_fusion = bf16[16,512,512]{2,1,0:T(8,128)(2,1)} fusion(bf16[16,512,512]{2,1,0:T(8,128)(2,1)} %gather_fusion.2, bf16[1,1,512,512]{3,2,1,0:T(8,128)(2,1)S(1)} %copy-done.3), kind=kOutput, calls=%fused_computation.10 | convolution fusion | flops 4299161600 | bytes 17301504 | tf_op jit(solution)/shard_map/ptik,tkl->pil/dot_general | solution.py:40
  294.1 0.0 reduce-scatter.2.cloned.1.call-update
  294.2 0.1 compare_select_fusion.2
  294.3 0.5 copy-done.2
  294.8 0.6 gather_fusion
  295.4 0.1 iota_compare_fusion.1
  295.5 88.4 %reduce-scatter.2.cloned.1.call-done = bf16[4,512,512]{2,1,0:T(8,128)(2,1)} async-done(((bf16[16,512,512]{2,1,0:T(8,128)(2,1)}), bf16[4,512,512]{2,1,0:T(8,128)(2,1)}) %reduce-scatter.2.cloned.1.call-update) | async-done | bytes 2097168 | tf_op jit(solution)/shard_map/reduce_scatter | solution.py:44
  383.9 3.0 fusion.8
  (7 shorter events, 0.0 us)
Async XLA Ops:
  6.5 4.0 %copy-start = (bf16[1,1,512,512]{3,2,1,0:T(8,128)(2,1)S(1)}, bf16[1,1,512,512]{3,2,1,0:T(8,128)(2,1)}, u32[]{:S(2)}) copy-start(bf16[1,1,512,512]{3,2,1,0:T(8,128)(2,1)} %param.6) | copy-start | bytes 1572868
  62.9 210.5 %all-to-all-start = ((bf16[32,1,512,512]{3,2,1,0:T(8,128)(2,1)}), bf16[32,1,512,512]{3,2,1,0:T(8,128)(2,1)}, u32[]{:S(2)}, u32[]{:S(2)}) async-start(bf16[32,1,512,512]{3,2,1,0:T(8,128)(2,1)} %bitcast.29), calls=%async_computation | async-start | bytes 33554432 | tf_op jit(solution)/shard_map/all_to_all | solution.py:9
  71.4 312.5 %reduce-scatter.2.cloned.1.call-start = ((), (), s32[]{:S(2)}) async-start(), calls=%async_computation.2 | async-start | bytes 10485760 | tf_op jit(solution)/shard_map/reduce_scatter | solution.py:44
  273.4 10.6 %copy-start.3 = (bf16[1,1,512,512]{3,2,1,0:T(8,128)(2,1)S(1)}, bf16[1,1,512,512]{3,2,1,0:T(8,128)(2,1)}, u32[]{:S(2)}) copy-start(bf16[1,1,512,512]{3,2,1,0:T(8,128)(2,1)} %param.7) | copy-start | bytes 1572868
  284.0 102.9 %copy-start.1 = (bf16[1,1,512,512]{3,2,1,0:T(8,128)(2,1)S(1)}, bf16[1,1,512,512]{3,2,1,0:T(8,128)(2,1)}, u32[]{:S(2)}) copy-start(bf16[1,1,512,512]{3,2,1,0:T(8,128)(2,1)} %param.6) | copy-start | bytes 1572868
  294.1 0.7 copy-start.2
Sparse Core Ops, SparseCore 0:
  294.3 89.5 reduce-scatter.1
where the time goes:
time: 395 us; the launch traced here: 394 us
  waiting for transfers between devices  290 us (73%)
  local copies, waits for them, and re-layouts  54 us (14%)
  matrix products  22.9 us (6%)
  between operations  13.4 us (3%)
  starting transfers between devices  8.58 us (2%)
  other arithmetic  4.54 us (1%)
    all_to_all x1, waiting for transfers between devices, relayout_blocks(): lax.all_to_all(outgoing, 'sec', split_axis=0, concat_axis=0, tiled=True)  202 us
    reduce_scatter x1, waiting for transfers between devices, body(): lax.psum_scatter(partial_value.astype(jnp.bfloat16), 'ops', scatter_dimen...  88.4 us
    scatter x1, local copies, waits for them, and re-layouts, relayout_blocks(): jnp.zeros((sectors,) + halfway.shape[1:], jnp.bfloat16).at[target]  21.4 us
    dot_general x1, matrix products, body(): jnp.einsum('tij,pjk->ptik', left_terms, blocks, preferred_element_type=jn...  12.7 us
    convert_element_type x1, local copies, waits for them, and re-layouts, body(): halfway = jnp.einsum('tij,pjk->ptik', left_terms, blocks, preferred_eleme...  12.3 us
    gather x1, local copies, waits for them, and re-layouts, relayout_blocks(): return arrived[anchor]  10.6 us
    dot_general x1, matrix products, body(): jnp.einsum('ptik,tkl->pil', incoming, right_terms, preferred_element_type...  10.2 us
    all_to_all x1, starting transfers between devices, relayout_blocks(): lax.all_to_all(outgoing, 'sec', split_axis=0, concat_axis=0, tiled=True)  8.54 us
  transfers between devices with their start and end apart: 2, of which 2 were waited for; matrix products, arithmetic and copies ran while one was open for 0% of the time, Pallas kernels for 0%

commit v1 on v0

v1 whole, which is shorter than its diff:
```python
import functools

import jax
import jax.numpy as jnp
from jax import lax
from jax.experimental import pallas as pl
from jax.experimental.pallas import tpu as pltpu
from jax.sharding import PartitionSpec as P

MESH = pl.DeviceIdType.MESH
BF16 = jnp.bfloat16
F32 = jnp.float32

M = 512
W = 128
C = M // W
NP = 16
H = W // 2

AG0, AG1, AG2, AG3, SIB = 0, 4, 8, 12, 16
RS, SWAP, A1, A2, ZOUT = 24, 30, 31, 37, 43
EVENTS = 46


class Copy:
    def __init__(self, make):
        self.make = make

    def start(self):
        self.make().start()

    def wait_send(self):
        self.make().wait_send()

    def wait_recv(self):
        self.make().wait_recv()


def kernel(shifts, dims, psi, left, right, out,
           inter, lmask, part, rsin, sigma, v, w, x0, x1, zbuf, inv,
           psem, osem, ssem, rsem, *chunked):
    rall, yf = chunked[:C], chunked[C:]
    g = lax.axis_index("ops")
    s = lax.axis_index("sec")
    y, x, c = s // 8, (s // 2) % 4, s % 2

    def dev(dz=0, dy=0, dx=0, dc=0):
        return ((g + dz) % 4, ((y + dy) % 4) * 8 + ((x + dx) % 4) * 2 + (c + dc) % 2)

    def copy(i, e, src, dst, to):
        return Copy(lambda: pltpu.make_async_remote_copy(
            src_ref=src, dst_ref=dst, send_sem=ssem.at[i, e], recv_sem=rsem.at[i, e],
            device_id=to, device_id_type=MESH))

    gp, gm, go = (g + 1) % 4, (g + 3) % 4, (g + 2) % 4
    xp, xm, xo = (x + 1) % 4, (x + 3) % 4, (x + 2) % 4
    yp, ym, yo = (y + 1) % 4, (y + 3) % 4, (y + 2) % 4
    XP, XM, YP, YM = dev(dx=1), dev(dx=3), dev(dy=1), dev(dy=3)
    ZP, ZM = dev(dz=1), dev(dz=3)
    SB = dev(dc=1)

    def ag0(i):
        a = rall[i].at[y, x, c, pl.ds(0, 256)]
        b = rall[i].at[y, x, c, pl.ds(256, 256)]
        return [copy(i, AG0, a, a, XP), copy(i, AG0 + 1, a, a, XM),
                copy(i, AG0 + 2, b, b, YP), copy(i, AG0 + 3, b, b, YM)]

    def ag1(i):
        q = [rall[i].at[y, xm, c, pl.ds(0, 128)], rall[i].at[y, xp, c, pl.ds(128, 128)],
             rall[i].at[ym, x, c, pl.ds(256, 128)], rall[i].at[yp, x, c, pl.ds(384, 128)]]
        return [copy(i, AG1 + k, r, r, to) for k, (r, to) in enumerate(zip(q, (XP, XM, YP, YM)))]

    def ag2(i):
        a = rall[i].at[y, :, c, pl.ds(0, 256)]
        b = rall[i].at[:, x, c, pl.ds(256, 256)]
        return [copy(i, AG2, a, a, YP), copy(i, AG2 + 1, a, a, YM),
                copy(i, AG2 + 2, b, b, XP), copy(i, AG2 + 3, b, b, XM)]

    def ag3(i):
        q = [rall[i].at[ym, :, c, pl.ds(0, 128)], rall[i].at[yp, :, c, pl.ds(128, 128)],
             rall[i].at[:, xm, c, pl.ds(256, 128)], rall[i].at[:, xp, c, pl.ds(384, 128)]]
        return [copy(i, AG3 + k, r, r, to) for k, (r, to) in enumerate(zip(q, (YP, YM, XP, XM)))]

    def sib(i):
        q = [rall[i].at[r, :, c, pl.ds(0, 256)] for r in (y, ym, yp, yo)]
        t = [rall[i].at[:, r, c, pl.ds(256, 256)] for r in (x, xm, xp, xo)]
        return [copy(i, SIB + k, r, r, SB) for k, r in enumerate(q + t)]

    def start(cs):
        for cp in cs:
            cp.start()

    def arrive(cs):
        for cp in cs:
            cp.wait_recv()

    def sent(cs):
        for cp in cs:
            cp.wait_send()

    def gather_step1(i):
        arrive(ag0(i))
        start(ag1(i))

    def gather_step2(i):
        arrive(ag1(i))
        start(ag2(i))
        cs = sib(i)
        start([cs[0], cs[4]])

    def gather_step3(i):
        arrive(ag2(i))
        start(ag3(i))
        cs = sib(i)
        start([cs[1], cs[2], cs[5], cs[6]])

    def gather_step4(i):
        arrive(ag3(i))
        cs = sib(i)
        start([cs[3], cs[7]])

    lo, hi = pl.ds(0, 8), pl.ds(8, 8)

    def rs(i):
        b = i % 2
        return [copy(i, RS, part.at[b, go, lo], rsin.at[i, 0], ZM),
                copy(i, RS + 1, part.at[b, go, hi], rsin.at[i, 1], ZP),
                copy(i, RS + 2, part.at[b, gp, lo], rsin.at[i, 2], ZP),
                copy(i, RS + 3, part.at[b, gm, hi], rsin.at[i, 3], ZM),
                copy(i, RS + 4, part.at[b, gm, lo], rsin.at[i, 4], ZM),
                copy(i, RS + 5, part.at[b, gp, hi], rsin.at[i, 5], ZP)]

    def products(i, first):
        b = i % 2

        @pl.loop(first, first + 8)
        def _(p):
            t = (s + shifts[p]) % 32
            r = jnp.dot(inter[p], rall[i][t // 8, (t // 2) % 4, t % 2], preferred_element_type=F32)
            r = r.astype(BF16)
            for d in range(4):
                part[b, d, p] = r[d * W:(d + 1) * W]

    def add_and_pass(i):
        b = i % 2
        cs = rs(i)
        cs[0].wait_recv()

        @pl.loop(0, 8)
        def _(p):
            part[b, gm, p] = (part[b, gm, p].astype(F32) + rsin[i, 0, p].astype(F32)).astype(BF16)

        cs[4].start()
        cs[1].wait_recv()

        @pl.loop(0, 8)
        def _(p):
            part[b, gp, p + 8] = (part[b, gp, p + 8].astype(F32) + rsin[i, 1, p].astype(F32)).astype(BF16)

        cs[5].start()

    def swap(i):
        return copy(i, SWAP, w.at[i], v.at[i, c], SB)

    def finish_sum(i):
        b = i % 2
        cs = rs(i)
        arrive(cs[2:])

        @pl.loop(0, 8)
        def _(p):
            sigma[p] = (part[b, g, p].astype(F32) + rsin[i, 2, p].astype(F32)
                        + rsin[i, 4, p].astype(F32)).astype(BF16)
            sigma[p + 8] = (part[b, g, p + 8].astype(F32) + rsin[i, 3, p].astype(F32)
                            + rsin[i, 5, p].astype(F32)).astype(BF16)

        @pl.loop(0, 16)
        def _(t):
            ty, tx = t // 4, t % 4
            base = ty * 8 + tx * 2 - s + 32
            w[i, ty, tx] = sigma[inv[(base + (c + 1) % 2) % 32]]
            v[i, c, ty, tx] = sigma[inv[(base + c) % 32]]

        swap(i).start()
        sent(cs)

    def a1(i):
        cs = []
        for d in (1, 3, 2):
            tx, ty = (x + d) % 4, (y + d) % 4
            cs.append(copy(i, A1 + d - 1, v.at[i, :, :, tx, pl.ds(0, H)], x0.at[i, x], dev(dx=d)))
            cs.append(copy(i, A1 + d + 2, v.at[i, :, ty, :, pl.ds(H, H)], x1.at[i, y], dev(dy=d)))
        return cs

    def a2(i):
        cs = []
        for d in (1, 3, 2):
            tx, ty = (x + d) % 4, (y + d) % 4
            cs.append(copy(i, A2 + d - 1, x0.at[i, :, :, ty], yf[i].at[y, :, :, pl.ds(0, H)], dev(dy=d)))
            cs.append(copy(i, A2 + d + 2, x1.at[i, :, :, tx], yf[i].at[:, x, :, pl.ds(H, H)], dev(dx=d)))
        return cs

    def exchange1(i):
        swap(i).wait_recv()
        start(a1(i))
        for k in range(4):
            for q in range(2):
                x0[i, x, q, k] = v[i, q, k, x, pl.ds(0, H)]
                x1[i, y, q, k] = v[i, q, y, k, pl.ds(H, H)]

    def exchange2(i):
        arrive(a1(i))
        start(a2(i))
        for k in range(4):
            for q in range(2):
                yf[i][y, k, q, pl.ds(0, H)] = x0[i, k, q, y]
                yf[i][k, x, q, pl.ds(H, H)] = x1[i, k, q, x]

    def place(i):
        return out.at[:, pl.ds(pl.multiple_of(g * W, W), W), pl.ds(i * W, W)]

    def zout(i):
        return [copy(i, ZOUT + d - 1, zbuf.at[i, (g + d) % 4], place(i), dev(dz=d)) for d in (2, 1, 3)]

    def own_out(i):
        return pltpu.make_async_copy(zbuf.at[i, g], place(i), osem.at[i])

    def exchange3(i):
        arrive(a2(i))

        @pl.loop(0, NP)
        def _(p):
            a = (s - shifts[p] + 32) % 32
            zbuf[i, p // 4, p % 4] = yf[i][a // 8, (a // 2) % 4, a % 2]

        start(zout(i))
        own_out(i).start()

    barrier = pltpu.get_barrier_semaphore()
    peers = ([dev(dz=d) for d in (1, 2, 3)] + [dev(dy=d) for d in (1, 2, 3)]
             + [dev(dx=d) for d in (1, 2, 3)] + [SB])
    for to in peers:
        pl.semaphore_signal(barrier, inc=1, device_id=to, device_id_type=MESH)

    def psi_copy(p):
        return pltpu.make_async_copy(psi.at[p], inter.at[p], psem.at[p])

    @pl.loop(0, NP)
    def _(p):
        psi_copy(p).start()

    own = dims[s]
    rows = lax.broadcasted_iota(jnp.int32, (M, W), 0)
    cols = lax.broadcasted_iota(jnp.int32, (M, W), 1)
    for i in range(C):
        live = (rows < own) & (cols + i * W < own)
        rall[i][y, x, c] = jnp.where(live, right[:, i * W:(i + 1) * W].astype(F32), 0.0).astype(BF16)
    pl.semaphore_wait(barrier, len(peers))
    start(ag0(0))
    for i in range(C):
        live = (rows < own) & (cols + i * W < own)
        lmask[:, i * W:(i + 1) * W] = jnp.where(live, left[:, i * W:(i + 1) * W].astype(F32), 0.0).astype(BF16)
    start(ag0(1))

    def find(k):
        r = jnp.int32(0)
        for p in range(NP):
            r = jnp.where(shifts[p] == k, jnp.int32(p), r)
        return r

    @pl.loop(0, 32)
    def _(k):
        inv[k] = find(k)

    def left_products(first, count):
        @pl.loop(first, first + count)
        def _(p):
            psi_copy(p).wait()
            for n in range(2):
                inter[p, :, n * 256:(n + 1) * 256] = jnp.dot(
                    lmask[...], inter[p, :, n * 256:(n + 1) * 256],
                    preferred_element_type=F32).astype(BF16)

    def g0(i):
        start(ag0(i))

    def lp(i):
        left_products(4 * i, 4)

    def pr(i):
        arrive(sib(i))
        products(i, 0)
        cs = rs(i)
        start([cs[0], cs[2]])
        products(i, 8)
        start([cs[1], cs[3]])

    g1, g2, g3, g4 = gather_step1, gather_step2, gather_step3, gather_step4
    ad, fi, e1, e2, e3 = add_and_pass, finish_sum, exchange1, exchange2, exchange3
    order = (
        (lp, 0), (g1, 0), (lp, 1), (g2, 0), (lp, 2), (g3, 0), (g1, 1), (lp, 3), (g2, 1), (g4, 0),
        (pr, 0), (g0, 2), (g3, 1), (g1, 2), (ad, 0), (g4, 1), (g2, 2), (pr, 1), (fi, 0),
        (g3, 2), (e1, 0), (ad, 1), (g4, 2), (e2, 0), (pr, 2), (g0, 3), (g1, 3), (fi, 1),
        (e3, 0), (e1, 1), (g2, 3), (ad, 2), (e2, 1), (g3, 3), (g4, 3), (pr, 3), (fi, 2),
        (e3, 1), (e1, 2), (ad, 3), (e2, 2), (fi, 3), (e3, 2), (e1, 3), (e2, 3), (e3, 3),
    )
    for step, i in order:
        step(i)

    for i in range(C):
        arrive(zout(i))
        own_out(i).wait()
        sent(ag0(i) + ag1(i) + ag2(i) + ag3(i) + sib(i) + [swap(i)] + a1(i) + a2(i) + zout(i))


def body(psi_blocks, left_env, right_env, shifts, sector_dims):
    vmem = pl.BlockSpec(memory_space=pltpu.VMEM)
    smem = pl.BlockSpec(memory_space=pltpu.SMEM)
    hbm = pl.BlockSpec(memory_space=pl.ANY)
    out = pl.pallas_call(
        kernel,
        name="sigma",
        out_shape=jax.ShapeDtypeStruct((4, M, M), BF16),
        in_specs=[smem, smem, hbm, vmem, vmem],
        out_specs=hbm,
        scratch_shapes=[
            pltpu.VMEM((NP, M, M), BF16),
            pltpu.VMEM((M, M), BF16),
            pltpu.VMEM((2, 4, NP, W, W), BF16),
            pltpu.VMEM((C, 6, 8, W, W), BF16),
            pltpu.VMEM((NP, W, W), BF16),
            pltpu.VMEM((C, 2, 4, 4, W, W), BF16),
            pltpu.VMEM((C, 4, 4, W, W), BF16),
            pltpu.VMEM((C, 4, 2, 4, H, W), BF16),
            pltpu.VMEM((C, 4, 2, 4, H, W), BF16),
            pltpu.VMEM((C, 4, 4, W, W), BF16),
            pltpu.SMEM((32,), jnp.int32),
            pltpu.SemaphoreType.DMA((NP,)),
            pltpu.SemaphoreType.DMA((C,)),
            pltpu.SemaphoreType.DMA((C, EVENTS)),
            pltpu.SemaphoreType.DMA((C, EVENTS)),
            *[pltpu.VMEM((4, 4, 2, M, W), BF16)] * C,
            *[pltpu.VMEM((4, 4, 2, W, W), BF16)] * C,
        ],
        compiler_params=pltpu.CompilerParams(
            collective_id=1, has_side_effects=True, vmem_limit_bytes=60 << 20),
        cost_estimate=pl.CostEstimate(flops=2 * 32 * M ** 3, bytes_accessed=12 << 20, transcendentals=0),
    )(shifts, sector_dims, psi_blocks[0], left_env[0, 0], right_env[0, 0])
    return out[None]


def solution(mesh):
    in_specs = (
        P("sec", None, None, None),
        P("ops", "sec", None, None),
        P("ops", "sec", None, None),
        P(),
        P(),
    )
    out_specs = P("sec", "ops", None, None)
    return jax.shard_map(body, mesh=mesh, in_specs=in_specs, out_specs=out_specs, check_vma=False)
```

time: 395 us -> 161 us (0.41)
  waiting for transfers between devices: 290 us -> 0 us
  Pallas kernels: 0 us -> 157 us
  local copies, waits for them, and re-layouts: 54 us -> 3.05 us
  matrix products: 22.9 us -> 0 us
  between operations: 13.4 us -> 0.01 us
  starting transfers between devices: 8.58 us -> 0 us
  other arithmetic: 4.54 us -> 0 us
    all_to_all x1 -> x0, waiting for transfers between devices: 202 us -> none  [relayout_blocks(): lax.all_to_all(outgoing, 'sec', split_axis=0, concat_axis=0, tiled=True)]
    pallas_call x0 -> x1, Pallas kernels: none -> 157 us  [body(): pl.pallas_call(kernel, name='sigma', out_shape=jax.ShapeDtypeStruct((4, M...]
    reduce_scatter x1 -> x0, waiting for transfers between devices: 88.4 us -> none  [body(): lax.psum_scatter(partial_value.astype(jnp.bfloat16), 'ops', scatter_dimen...]
    dot_general x2 -> x0, matrix products: 22.9 us -> none  [the longest x1 12.7 us: body(): jnp.einsum('tij,pjk->ptik', left_terms, blocks, preferred_element_type=jn...]
    scatter x1 -> x0, local copies, waits for them, and re-layouts: 21.4 us -> none  [relayout_blocks(): jnp.zeros((sectors,) + halfway.shape[1:], jnp.bfloat16).at[target]]
    gather x3 -> x0, local copies, waits for them, and re-layouts: 12.5 us -> none  [the longest x1 10.6 us: relayout_blocks(): return arrived[anchor]]
    convert_element_type x1 -> x0, local copies, waits for them, and re-layouts: 12.3 us -> none  [body(): halfway = jnp.einsum('tij,pjk->ptik', left_terms, blocks, preferred_eleme...]
    all_to_all x1 -> x0, starting transfers between devices: 8.54 us -> none  [relayout_blocks(): lax.all_to_all(outgoing, 'sec', split_axis=0, concat_axis=0, tiled=True)]
  transfers between devices with their start and end apart: 2 -> 0, of which waited for: 2 -> 0; matrix products, arithmetic and copies ran while one was open for 0% -> 0% of each run, Pallas kernels for 0% -> 0%
where the time goes in v1:
time: 161 us; the launch traced here: 160 us
  Pallas kernels  157 us (98%)
  local copies, waits for them, and re-layouts  3.05 us (2%)
    pallas_call x1, Pallas kernels, body(): pl.pallas_call(kernel, name='sigma', out_shape=jax.ShapeDtypeStruct((4, M...  157 us

profile of v1, /device:TPU:1, one launch (start us, length us, event | category | flops | bytes accessed | tf_op | source)
XLA Modules:
  0.0 160.1 jit_solution(14250774977547539967)
XLA Ops:
  0.0 157.0 %sigma.1 = bf16[4,512,512]{2,1,0:T(8,128)(2,1)} custom-call(s32[16]{0:T(128)} %shifts.1, s32[32]{0:T(128)} %dims.1, bf16[16,512,512]{2,1,0:T(8,128)(2,1)} %bitcast.5, bf16[512,512]{1,0:T(8,128)(2,1)} %bitcast.6, bf16[512,512]{1,0:T(8,128)(2,1)} %bitcast.7), custom_call_target="tpu_custom_call" | custom-call | flops 8589934592 | bytes 12582912 | tf_op jit(solution)/shard_map/sigma/pallas_call | solution.py:320
  157.0 3.0 %copy.7 = bf16[1,4,512,512]{3,2,1,0:T(8,128)(2,1)} copy(bf16[1,4,512,512]{3,2,1,0:T(8,128)(2,1)} %bitcast.4) | data formatting | bytes 4194304

commit v2 on v1

--- a/solution.py
+++ b/solution.py
@@ -133,7 +133,7 @@
     def products(i, first):
         b = i % 2
 
-        @pl.loop(first, first + 8)
+        @pl.loop(first, first + 8, unroll=8)
         def _(p):
             t = (s + shifts[p]) % 32
             r = jnp.dot(inter[p], rall[i][t // 8, (t // 2) % 4, t % 2], preferred_element_type=F32)
@@ -298,11 +298,12 @@
     g1, g2, g3, g4 = gather_step1, gather_step2, gather_step3, gather_step4
     ad, fi, e1, e2, e3 = add_and_pass, finish_sum, exchange1, exchange2, exchange3
     order = (
-        (lp, 0), (g1, 0), (lp, 1), (g2, 0), (lp, 2), (g3, 0), (g1, 1), (lp, 3), (g2, 1), (g4, 0),
-        (pr, 0), (g0, 2), (g3, 1), (g1, 2), (ad, 0), (g4, 1), (g2, 2), (pr, 1), (fi, 0),
-        (g3, 2), (e1, 0), (ad, 1), (g4, 2), (e2, 0), (pr, 2), (g0, 3), (g1, 3), (fi, 1),
-        (e3, 0), (e1, 1), (g2, 3), (ad, 2), (e2, 1), (g3, 3), (g4, 3), (pr, 3), (fi, 2),
-        (e3, 1), (e1, 2), (ad, 3), (e2, 2), (fi, 3), (e3, 2), (e1, 3), (e2, 3), (e3, 3),
+        (lp, 1), (g1, 0), (g0, 2), (lp, 3), (g2, 0), (g1, 1), (g1, 2), (g3, 0), (lp, 2),
+        (lp, 0), (g4, 0), (g2, 1), (g2, 2), (pr, 0), (g3, 1), (g0, 3), (ad, 0), (g1, 3),
+        (g4, 1), (g3, 2), (pr, 1), (g4, 2), (fi, 0), (e1, 0), (g2, 3), (pr, 2), (g3, 3),
+        (ad, 1), (g4, 3), (e2, 0), (ad, 2), (fi, 1), (pr, 3), (e1, 1), (fi, 2), (e1, 2),
+        (e2, 1), (ad, 3), (e2, 2), (fi, 3), (e3, 0), (e1, 3), (e3, 2), (e2, 3), (e3, 1),
+        (e3, 3),
     )
     for step, i in order:
         step(i)

time: 161 us -> 138 us (0.86)
  Pallas kernels: 157 us -> 135 us
    pallas_call x1, Pallas kernels: 157 us -> 135 us  [body(): pl.pallas_call(kernel, name='sigma', out_shape=jax.ShapeDtypeStruct((4, M...]
where the time goes in v2:
time: 138 us
  Pallas kernels  135 us (98%)
  local copies, waits for them, and re-layouts  3.05 us (2%)
    pallas_call x1, Pallas kernels, body(): pl.pallas_call(kernel, name='sigma', out_shape=jax.ShapeDtypeStruct((4, M...  135 us
    unnamed x1, local copies, waits for them, and re-layouts  3.05 us

profile of v2, /device:TPU:1, one launch (start us, length us, event | category | flops | bytes accessed | tf_op | source)
XLA Modules:
  0.0 137.6 jit_solution(3479331333990344967)
XLA Ops:
  0.0 134.6 %sigma.1 = bf16[4,512,512]{2,1,0:T(8,128)(2,1)} custom-call(s32[16]{0:T(128)} %shifts.1, s32[32]{0:T(128)} %dims.1, bf16[16,512,512]{2,1,0:T(8,128)(2,1)} %bitcast.5, bf16[512,512]{1,0:T(8,128)(2,1)} %bitcast.6, bf16[512,512]{1,0:T(8,128)(2,1)} %bitcast.7), custom_call_target="tpu_custom_call" | custom-call | flops 8589934592 | bytes 12582912 | tf_op jit(solution)/shard_map/sigma/pallas_call | solution.py:321
  134.6 3.0 %copy.7 = bf16[1,4,512,512]{3,2,1,0:T(8,128)(2,1)} copy(bf16[1,4,512,512]{3,2,1,0:T(8,128)(2,1)} %bitcast.4) | data formatting | bytes 4194304

commit v3 on v0

v3 whole, which is shorter than its diff:
```python
import jax
import jax.numpy as jnp
from jax import lax
from jax.experimental import pallas as pl
from jax.experimental.pallas import tpu as pltpu
from jax.sharding import PartitionSpec as P

MESH = pl.DeviceIdType.MESH
BF16 = jnp.bfloat16
F32 = jnp.float32

M = 512
W = 128
C = M // W
NP = 16
H = W // 2
Q = H // 2
U = 2 * C
NR = NP - 2
HALF = NR // 2

AG0, AG1, AG2, AG3, SIB = 0, 4, 8, 20, 32
GATHER = 38
RS, SWAP, A1, A2, ZOUT = 0, 6, 7, 13, 19
UNIT = 22


class Copy:
    def __init__(self, make):
        self.make = make

    def start(self):
        self.make().start()

    def wait_send(self):
        self.make().wait_send()

    def wait_recv(self):
        self.make().wait_recv()


def start(cs):
    for cp in cs:
        cp.start()


def arrive(cs):
    for cp in cs:
        cp.wait_recv()


def sent(cs):
    for cp in cs:
        cp.wait_send()


def kernel(shifts, dims, psi, left, right, out,
           inter, early, lmask, rmask, rnext, part, part0, rsin, rsin0, sigma, sigma0,
           v, w, x0, x1, zbuf, inv, place_of,
           psem, lsem, osem, gsend, grecv, usend, urecv, *chunked):
    rall, yf = chunked[:C], chunked[C:]
    g = lax.axis_index("ops")
    s = lax.axis_index("sec")
    y, x, c = s // 8, (s // 2) % 4, s % 2

    def dev(dz=0, dy=0, dx=0, dc=0):
        return ((g + dz) % 4, ((y + dy) % 4) * 8 + ((x + dx) % 4) * 2 + (c + dc) % 2)

    def copy(sems, i, e, src, dst, to):
        return Copy(lambda: pltpu.make_async_remote_copy(
            src_ref=src, dst_ref=dst, send_sem=sems[0].at[i, e], recv_sem=sems[1].at[i, e],
            device_id=to, device_id_type=MESH))

    GS, US = (gsend, grecv), (usend, urecv)
    gp, gm, go = (g + 1) % 4, (g + 3) % 4, (g + 2) % 4
    xp, xm, xo = (x + 1) % 4, (x + 3) % 4, (x + 2) % 4
    yp, ym, yo = (y + 1) % 4, (y + 3) % 4, (y + 2) % 4
    XP, XM, YP, YM = dev(dx=1), dev(dx=3), dev(dy=1), dev(dy=3)
    ZP, ZM = dev(dz=1), dev(dz=3)
    SB = dev(dc=1)

    def tile(i, yy, xx, first, count):
        return rall[i].at[yy // 2, yy % 2, xx // 2, xx % 2, c, pl.ds(first, count)]

    def row(i, yy, kind, first, count):
        yh, yl = yy // 2, yy % 2
        if kind == "all":
            return rall[i].at[yh, yl, :, :, c, pl.ds(first, count)]
        return rall[i].at[yh, yl, :, (x + 1) % 2, c, pl.ds(first, count)]

    def col(i, xx, kind, first, count):
        xh, xl = xx // 2, xx % 2
        if kind == "all":
            return rall[i].at[:, :, xh, xl, c, pl.ds(first, count)]
        return rall[i].at[:, (y + 1) % 2, xh, xl, c, pl.ds(first, count)]

    def four(i, e, refs, to):
        return [copy(GS, i, e + k, r, r, d) for k, (r, d) in enumerate(zip(refs, to))]

    def ag0(i):
        a, b = tile(i, y, x, 0, 256), tile(i, y, x, 256, 256)
        return four(i, AG0, (a, a, b, b), (XP, XM, YP, YM))

    def ag1(i):
        return four(i, AG1, (tile(i, y, xm, 0, 128), tile(i, y, xp, 128, 128),
                             tile(i, ym, x, 256, 128), tile(i, yp, x, 384, 128)), (XP, XM, YP, YM))

    def ag2a(i):
        a, b = tile(i, y, x, 0, 256), tile(i, y, x, 256, 256)
        return four(i, AG2, (a, a, b, b), (YP, YM, XP, XM))

    def ag2b(i):
        a, b = row(i, y, "near", 0, 256), col(i, x, "near", 256, 256)
        return four(i, AG2 + 4, (a, a, b, b), (YP, YM, XP, XM))

    def ag2c(i):
        a, b = tile(i, y, xo, 0, 256), tile(i, yo, x, 256, 256)
        return four(i, AG2 + 8, (a, a, b, b), (YP, YM, XP, XM))

    def ag3a(i):
        return four(i, AG3, (tile(i, ym, x, 0, 128), tile(i, yp, x, 128, 128),
                             tile(i, y, xm, 256, 128), tile(i, y, xp, 384, 128)), (YP, YM, XP, XM))

    def ag3b(i):
        return four(i, AG3 + 4, (row(i, ym, "near", 0, 128), row(i, yp, "near", 128, 128),
                                 col(i, xm, "near", 256, 128), col(i, xp, "near", 384, 128)),
                    (YP, YM, XP, XM))

    def ag3c(i):
        return four(i, AG3 + 8, (tile(i, ym, xo, 0, 128), tile(i, yp, xo, 128, 128),
                                 tile(i, yo, xm, 256, 128), tile(i, yo, xp, 384, 128)),
                    (YP, YM, XP, XM))

    def sib(i):
        refs = (row(i, y, "all", 0, 256), col(i, x, "all", 256, 256),
                rall[i].at[:, (y + 1) % 2, :, :, c, pl.ds(0, 256)],
                rall[i].at[:, :, :, (x + 1) % 2, c, pl.ds(256, 256)],
                row(i, yo, "all", 0, 256), col(i, xo, "all", 256, 256))
        return [copy(GS, i, SIB + k, r, r, SB) for k, r in enumerate(refs)]

    def g0(i):
        start(ag0(i) + ag2a(i))

    def g1(i):
        arrive(ag0(i))
        start(ag1(i) + ag2b(i))

    def g2(i):
        arrive(ag1(i))
        start(ag2c(i) + sib(i)[:2])

    def ga(i):
        arrive(ag2a(i) + ag2b(i))
        start(ag3a(i) + ag3b(i))

    def g3(i):
        arrive(ag2c(i))
        start(ag3c(i) + sib(i)[2:4])

    def g4(i):
        arrive(ag3a(i) + ag3b(i) + ag3c(i))
        start(sib(i)[4:])

    def psi_copy(p):
        return pltpu.make_async_copy(psi.at[p], inter.at[p], psem.at[p])

    def lp(i):
        @pl.loop(4 * i, 4 * i + 4)
        def _(p):
            inter[p] = jnp.dot(lmask[...], inter[p], preferred_element_type=F32).astype(BF16)

    def passes(u, send_a, send_b, into, a, b):
        return [copy(US, u, RS, send_a(go), into(0, a), ZM), copy(US, u, RS + 1, send_b(go), into(1, b), ZP),
                copy(US, u, RS + 2, send_a(gp), into(2, a), ZP), copy(US, u, RS + 3, send_b(gm), into(3, b), ZM),
                copy(US, u, RS + 4, send_a(gm), into(4, a), ZM), copy(US, u, RS + 5, send_b(gp), into(5, b), ZP)]

    def rs(u):
        b, r = (u // 2) % 2, pl.ds((u % 2) * H, H)
        return passes(u, lambda d: part.at[b, d, pl.ds(0, HALF), r], lambda d: part.at[b, d, pl.ds(HALF, HALF), r],
                      lambda k, _: rsin.at[u, k], 0, 1)

    def rs0():
        return passes(U, lambda d: part0.at[d, 0], lambda d: part0.at[d, 1], lambda k, _: rsin0.at[k], 0, 1)

    def products(i, first):
        b = i % 2

        @pl.loop(first, first + HALF, unroll=HALF)
        def _(j):
            p = j + (j >= place_of[0]).astype(jnp.int32)
            p = p + (p >= place_of[1]).astype(jnp.int32)
            t = (s + shifts[p]) % 32
            r = jnp.dot(inter[p], rall[i][t // 16, (t // 8) % 2, (t // 4) % 2, (t // 2) % 2, t % 2],
                        preferred_element_type=F32).astype(BF16)
            for d in range(4):
                part[b, d, j] = r[d * W:(d + 1) * W]

    def pr(i):
        arrive(sib(i))
        cs = rs(2 * i)
        products(i, 0)
        start([cs[0], cs[2]])
        products(i, HALF)
        start([cs[1], cs[3]])

    def ps(i):
        start(rs(2 * i + 1)[:4])

    def ad(u):
        b, r = (u // 2) % 2, slice((u % 2) * H, (u % 2) * H + H)
        cs = rs(u)
        for k, d, first in ((0, gm, 0), (1, gp, HALF)):
            cs[k].wait_recv()

            @pl.loop(0, HALF, unroll=HALF)
            def _(j):
                part[b, d, first + j, r] = (part[b, d, first + j, r].astype(F32)
                                            + rsin[u, k, j].astype(F32)).astype(BF16)

            cs[4 + k].start()

    def swap(u):
        return copy(US, u, SWAP, w.at[u], v.at[u, c], SB)

    def fi(u):
        i, r = u // 2, slice((u % 2) * H, (u % 2) * H + H)
        b = i % 2
        cs = rs(u)
        arrive(cs[2:])

        @pl.loop(0, HALF, unroll=HALF)
        def _(j):
            sigma[j] = (part[b, g, j, r].astype(F32) + rsin[u, 2, j].astype(F32)
                        + rsin[u, 4, j].astype(F32)).astype(BF16)
            sigma[j + HALF] = (part[b, g, j + HALF, r].astype(F32) + rsin[u, 3, j].astype(F32)
                               + rsin[u, 5, j].astype(F32)).astype(BF16)

        sigma[NR] = sigma0[0, i, r]
        sigma[NR + 1] = sigma0[1, i, r]

        @pl.loop(0, 16, unroll=4)
        def _(t):
            ty, tx = t // 4, t % 4
            base = ty * 8 + tx * 2 - s + 32
            w[u, ty, tx] = sigma[inv[(base + (c + 1) % 2) % 32]]
            v[u, c, ty, tx] = sigma[inv[(base + c) % 32]]

        swap(u).start()
        sent(cs)

    def next_right():
        return copy(US, U, SWAP, rmask, rnext, SB)

    def s0(_):
        @pl.loop(0, NP)
        def _(p):
            psi_copy(p).wait()

        cs = rs0()
        for k, ref in ((0, rmask), (1, rnext)):
            if k:
                next_right().wait_recv()
            early[...] = jnp.dot(lmask[...], inter[place_of[2 + k]], preferred_element_type=F32).astype(BF16)
            r = jnp.dot(early[...], ref[...], preferred_element_type=F32).astype(BF16)
            for d in range(4):
                for i in range(C):
                    part0[d, k, i] = r[d * W:(d + 1) * W, i * W:(i + 1) * W]
            start([cs[k], cs[2 + k]])

    def s1(_):
        cs = rs0()
        for k, d in ((0, gm), (1, gp)):
            cs[k].wait_recv()
            for i in range(C):
                part0[d, k, i] = (part0[d, k, i].astype(F32) + rsin0[k, i].astype(F32)).astype(BF16)
            cs[4 + k].start()

    def s2(_):
        cs = rs0()
        arrive(cs[2:])
        for k in range(2):
            for i in range(C):
                sigma0[k, i] = (part0[g, k, i].astype(F32) + rsin0[2 + k, i].astype(F32)
                                + rsin0[4 + k, i].astype(F32)).astype(BF16)

    def a1(u):
        cs = []
        for d in (1, 3, 2):
            tx, ty = (x + d) % 4, (y + d) % 4
            cs.append(copy(US, u, A1 + d - 1, v.at[u, :, :, tx, pl.ds(0, Q)], x0.at[u, x], dev(dx=d)))
            cs.append(copy(US, u, A1 + d + 2, v.at[u, :, ty, :, pl.ds(Q, Q)], x1.at[u, y], dev(dy=d)))
        return cs

    def a2(u):
        cs = []
        for d in (1, 3, 2):
            tx, ty = (x + d) % 4, (y + d) % 4
            cs.append(copy(US, u, A2 + d - 1, x0.at[u, :, :, ty], yf[u].at[y, :, :, pl.ds(0, Q)], dev(dy=d)))
            cs.append(copy(US, u, A2 + d + 2, x1.at[u, :, :, tx], yf[u].at[:, x, :, pl.ds(Q, Q)], dev(dx=d)))
        return cs

    def e1(u):
        swap(u).wait_recv()
        start(a1(u))
        for k in range(4):
            for q in range(2):
                x0[u, x, q, k] = v[u, q, k, x, pl.ds(0, Q)]
                x1[u, y, q, k] = v[u, q, y, k, pl.ds(Q, Q)]

    def e2(u):
        arrive(a1(u))
        start(a2(u))
        for k in range(4):
            for q in range(2):
                yf[u][y, k, q, pl.ds(0, Q)] = x0[u, k, q, y]
                yf[u][k, x, q, pl.ds(Q, Q)] = x1[u, k, q, x]

    def place(u):
        return out.at[:, pl.ds(pl.multiple_of(g * W + (u % 2) * H, H), H), pl.ds((u // 2) * W, W)]

    def zout(u):
        return [copy(US, u, ZOUT + d - 1, zbuf.at[u, (g + d) % 4], place(u), dev(dz=d)) for d in (2, 1, 3)]

    def own_out(u):
        return pltpu.make_async_copy(zbuf.at[u, g], place(u), osem.at[u])

    def e3(u):
        arrive(a2(u))

        @pl.loop(0, NP, unroll=4)
        def _(p):
            a = (s - shifts[p] + 32) % 32
            zbuf[u, p // 4, p % 4] = yf[u][a // 8, (a // 2) % 4, a % 2]

        start(zout(u))
        own_out(u).start()

    barrier = pltpu.get_barrier_semaphore()
    peers = ([dev(dz=d) for d in (1, 2, 3)] + [dev(dy=d) for d in (1, 2, 3)]
             + [dev(dx=d) for d in (1, 2, 3)] + [SB])
    for to in peers:
        pl.semaphore_signal(barrier, inc=1, device_id=to, device_id_type=MESH)

    def right_copy(i):
        cols = pl.ds(i * W, W)
        return pltpu.make_async_copy(right.at[:, cols], rmask.at[:, cols], lsem.at[i])

    left_copy = Copy(lambda: pltpu.make_async_copy(left, lmask, lsem.at[C]))
    for i in range(C):
        right_copy(i).start()
    left_copy.start()

    @pl.loop(0, NP)
    def _(p):
        psi_copy(p).start()

    own = dims[s]
    rows = lax.broadcasted_iota(jnp.int32, (M, W), 0)
    cols = lax.broadcasted_iota(jnp.int32, (M, W), 1)

    def masked(ref, i):
        live = (rows < own) & (cols + i * W < own)
        return jnp.where(live, ref[:, i * W:(i + 1) * W].astype(F32), 0.0).astype(BF16)

    def own_right(i):
        right_copy(i).wait()
        r = masked(rmask, i)
        rmask[:, i * W:(i + 1) * W] = r
        rall[i][y // 2, y % 2, x // 2, x % 2, c] = r

    own_right(0)
    pl.semaphore_wait(barrier, len(peers))
    g0(0)
    for i in range(1, C):
        own_right(i)
    next_right().start()
    pltpu.make_async_copy(left, lmask, lsem.at[C]).wait()
    for i in range(C):
        lmask[:, i * W:(i + 1) * W] = masked(lmask, i)

    def slot_of(k):
        r = jnp.int32(0)
        for p in range(NP):
            r = jnp.where(shifts[p] == k, jnp.int32(p), r)
        return r

    pa, pb = slot_of(0), slot_of(1 + 30 * c)
    low, high = jnp.minimum(pa, pb), jnp.maximum(pa, pb)
    place_of[0] = low
    place_of[1] = high
    place_of[2] = pa
    place_of[3] = pb

    @pl.loop(0, 32)
    def _(k):
        p = slot_of(k)
        r = p - (p > low).astype(jnp.int32) - (p > high).astype(jnp.int32)
        r = jnp.where(p == pa, jnp.int32(NR), r)
        inv[k] = jnp.where(p == pb, jnp.int32(NR + 1), r)

    order = (
        (g1, 0), (s0, 0), (g2, 0), (lp, 1), (ga, 0), (lp, 3), (g3, 0), (g0, 1), (s1, 0),
        (lp, 2), (g4, 0), (g1, 1), (lp, 0), (g0, 3), (pr, 0), (s2, 0), (g2, 1), (g0, 2),
        (ga, 1), (ps, 0), (g3, 1), (ad, 0), (g1, 2), (g4, 1), (g2, 2), (ad, 1), (g1, 3),
        (pr, 1), (fi, 0), (ps, 1), (ga, 2), (g3, 2), (g2, 3), (ad, 2), (ga, 3), (g4, 2),
        (e1, 0), (fi, 1), (g3, 3), (ad, 3), (pr, 2), (ps, 2), (fi, 2), (e1, 1), (g4, 3),
        (e2, 0), (fi, 3), (e2, 1), (ad, 4), (pr, 3), (e1, 3), (e1, 2), (ad, 5), (fi, 4),
        (e1, 4), (ps, 3), (e2, 3), (fi, 5), (ad, 6), (e3, 0), (e2, 4), (e1, 5), (ad, 7),
        (e2, 2), (e3, 3), (e2, 5), (fi, 6), (e1, 6), (e3, 1), (fi, 7), (e1, 7), (e3, 5),
        (e3, 4), (e3, 2), (e2, 6), (e2, 7), (e3, 6), (e3, 7),
    )
    for step, i in order:
        step(i)

    for u in range(U):
        arrive(zout(u))
        own_out(u).wait()

    for i in range(C):
        sent(ag0(i) + ag1(i) + ag2a(i) + ag2b(i) + ag2c(i) + ag3a(i) + ag3b(i) + ag3c(i) + sib(i))
    for u in range(U):
        sent([swap(u)] + a1(u) + a2(u) + zout(u))
    sent([next_right()] + rs0())


def body(psi_blocks, left_env, right_env, shifts, sector_dims):
    smem = pl.BlockSpec(memory_space=pltpu.SMEM)
    hbm = pl.BlockSpec(memory_space=pl.ANY)
    out = pl.pallas_call(
        kernel,
        name="sigma",
        out_shape=jax.ShapeDtypeStruct((4, M, M), BF16),
        in_specs=[smem, smem, hbm, hbm, hbm],
        out_specs=hbm,
        scratch_shapes=[
            pltpu.VMEM((NP, M, M), BF16),
            pltpu.VMEM((M, M), BF16),
            pltpu.VMEM((M, M), BF16),
            pltpu.VMEM((M, M), BF16),
            pltpu.VMEM((M, M), BF16),
            pltpu.VMEM((2, 4, NR, W, W), BF16),
            pltpu.VMEM((4, 2, C, W, W), BF16),
            pltpu.VMEM((U, 6, HALF, H, W), BF16),
            pltpu.VMEM((6, C, W, W), BF16),
            pltpu.VMEM((NP, H, W), BF16),
            pltpu.VMEM((2, C, W, W), BF16),
            pltpu.VMEM((U, 2, 4, 4, H, W), BF16),
            pltpu.VMEM((U, 4, 4, H, W), BF16),
            pltpu.VMEM((U, 4, 2, 4, Q, W), BF16),
            pltpu.VMEM((U, 4, 2, 4, Q, W), BF16),
            pltpu.VMEM((U, 4, 4, H, W), BF16),
            pltpu.SMEM((32,), jnp.int32),
            pltpu.SMEM((4,), jnp.int32),
            pltpu.SemaphoreType.DMA((NP,)),
            pltpu.SemaphoreType.DMA((C + 1,)),
            pltpu.SemaphoreType.DMA((U,)),
            pltpu.SemaphoreType.DMA((C, GATHER)),
            pltpu.SemaphoreType.DMA((C, GATHER)),
            pltpu.SemaphoreType.DMA((U + 1, UNIT)),
            pltpu.SemaphoreType.DMA((U + 1, UNIT)),
            *[pltpu.VMEM((2, 2, 2, 2, 2, M, W), BF16)] * C,
            *[pltpu.VMEM((4, 4, 2, H, W), BF16)] * U,
        ],
        compiler_params=pltpu.CompilerParams(
            collective_id=1, has_side_effects=True, vmem_limit_bytes=60 << 20),
        cost_estimate=pl.CostEstimate(flops=2 * 32 * M ** 3, bytes_accessed=12 << 20, transcendentals=0),
    )(shifts, sector_dims, psi_blocks[0], left_env[0, 0], right_env[0, 0])
    return out[None]


def solution(mesh):
    in_specs = (
        P("sec", None, None, None),
        P("ops", "sec", None, None),
        P("ops", "sec", None, None),
        P(),
        P(),
    )
    out_specs = P("sec", "ops", None, None)
    return jax.shard_map(body, mesh=mesh, in_specs=in_specs, out_specs=out_specs, check_vma=False)
```

time: 395 us -> 123 us (0.31)
  waiting for transfers between devices: 290 us -> 0 us
  Pallas kernels: 0 us -> 119 us
  local copies, waits for them, and re-layouts: 54 us -> 3.05 us
  matrix products: 22.9 us -> 0 us
  between operations: 13.4 us -> 0.01 us
  starting transfers between devices: 8.58 us -> 0 us
  other arithmetic: 4.54 us -> 0 us
    all_to_all x1 -> x0, waiting for transfers between devices: 202 us -> none  [relayout_blocks(): lax.all_to_all(outgoing, 'sec', split_axis=0, concat_axis=0, tiled=True)]
    pallas_call x0 -> x1, Pallas kernels: none -> 119 us  [body(): pl.pallas_call(kernel, name='sigma', out_shape=jax.ShapeDtypeStruct((4, M...]
    reduce_scatter x1 -> x0, waiting for transfers between devices: 88.4 us -> none  [body(): lax.psum_scatter(partial_value.astype(jnp.bfloat16), 'ops', scatter_dimen...]
    dot_general x2 -> x0, matrix products: 22.9 us -> none  [the longest x1 12.7 us: body(): jnp.einsum('tij,pjk->ptik', left_terms, blocks, preferred_element_type=jn...]
    scatter x1 -> x0, local copies, waits for them, and re-layouts: 21.4 us -> none  [relayout_blocks(): jnp.zeros((sectors,) + halfway.shape[1:], jnp.bfloat16).at[target]]
    gather x3 -> x0, local copies, waits for them, and re-layouts: 12.5 us -> none  [the longest x1 10.6 us: relayout_blocks(): return arrived[anchor]]
    convert_element_type x1 -> x0, local copies, waits for them, and re-layouts: 12.3 us -> none  [body(): halfway = jnp.einsum('tij,pjk->ptik', left_terms, blocks, preferred_eleme...]
    all_to_all x1 -> x0, starting transfers between devices: 8.54 us -> none  [relayout_blocks(): lax.all_to_all(outgoing, 'sec', split_axis=0, concat_axis=0, tiled=True)]
  transfers between devices with their start and end apart: 2 -> 0, of which waited for: 2 -> 0; matrix products, arithmetic and copies ran while one was open for 0% -> 0% of each run, Pallas kernels for 0% -> 0%
where the time goes in v3:
time: 123 us; the launch traced here: 122 us
  Pallas kernels  119 us (97%)
  local copies, waits for them, and re-layouts  3.05 us (2%)
    pallas_call x1, Pallas kernels, body(): pl.pallas_call(kernel, name='sigma', out_shape=jax.ShapeDtypeStruct((4, M...  119 us
    unnamed x1, local copies, waits for them, and re-layouts  3.05 us

profile of v3, /device:TPU:1, one launch (start us, length us, event | category | flops | bytes accessed | tf_op | source)
XLA Modules:
  0.0 122.4 jit_solution(1267468000594775705)
XLA Ops:
  0.0 119.3 %sigma.1 = bf16[4,512,512]{2,1,0:T(8,128)(2,1)} custom-call(s32[16]{0:T(128)} %shifts.1, s32[32]{0:T(128)} %dims.1, bf16[16,512,512]{2,1,0:T(8,128)(2,1)} %bitcast.5, bf16[512,512]{1,0:T(8,128)(2,1)} %bitcast.6, bf16[512,512]{1,0:T(8,128)(2,1)} %bitcast.7), custom_call_target="tpu_custom_call" | custom-call | flops 8589934592 | bytes 12582912 | tf_op jit(solution)/shard_map/sigma/pallas_call | solution.py:429
  119.3 3.0 %copy.7 = bf16[1,4,512,512]{3,2,1,0:T(8,128)(2,1)} copy(bf16[1,4,512,512]{3,2,1,0:T(8,128)(2,1)} %bitcast.4) | data formatting | bytes 4194304

commit v4 on v3

--- a/solution.py
+++ b/solution.py
@@ -19,10 +19,10 @@
 NR = NP - 2
 HALF = NR // 2
 
-AG0, AG1, AG2, AG3, SIB = 0, 4, 8, 20, 32
-GATHER = 38
-RS, SWAP, A1, A2, ZOUT = 0, 6, 7, 13, 19
-UNIT = 22
+AG0, AG1, AG2, AG2C, AG3, SIB = range(6)
+GATHER = 6
+RS, RSB, RSC, SWAP, A1, A2, ZOUT = range(7)
+UNIT = 7
 
 
 class Copy:
@@ -32,9 +32,6 @@
     def start(self):
         self.make().start()
 
-    def wait_send(self):
-        self.make().wait_send()
-
     def wait_recv(self):
         self.make().wait_recv()
 
@@ -44,20 +41,10 @@
         cp.start()
 
 
-def arrive(cs):
-    for cp in cs:
-        cp.wait_recv()
-
-
-def sent(cs):
-    for cp in cs:
-        cp.wait_send()
-
-
 def kernel(shifts, dims, psi, left, right, out,
            inter, early, lmask, rmask, rnext, part, part0, rsin, rsin0, sigma, sigma0,
            v, w, x0, x1, zbuf, inv, place_of,
-           psem, lsem, osem, gsend, grecv, usend, urecv, *chunked):
+           psem, lsem, osem, gsend, grecv, rsend, xsend, urecv, *chunked):
     rall, yf = chunked[:C], chunked[C:]
     g = lax.axis_index("ops")
     s = lax.axis_index("sec")
@@ -66,18 +53,27 @@
     def dev(dz=0, dy=0, dx=0, dc=0):
         return ((g + dz) % 4, ((y + dy) % 4) * 8 + ((x + dx) % 4) * 2 + (c + dc) % 2)
 
-    def copy(sems, i, e, src, dst, to):
+    SB = dev(dc=1)
+
+    def copy(send, recv, src, dst, to):
         return Copy(lambda: pltpu.make_async_remote_copy(
-            src_ref=src, dst_ref=dst, send_sem=sems[0].at[i, e], recv_sem=sems[1].at[i, e],
-            device_id=to, device_id_type=MESH))
-
-    GS, US = (gsend, grecv), (usend, urecv)
+            src_ref=src, dst_ref=dst, send_sem=send, recv_sem=recv, device_id=to, device_id_type=MESH))
+
+    def take(sem, kib, received=True):
+        n = next(n for n in range(1, NP + 1) if kib <= n * M and kib % (16 * n) == 0)
+        view = inter.at[pl.ds(0, n), pl.ds(0, kib // n)]
+        cp = pltpu.make_async_remote_copy(
+            src_ref=view, dst_ref=view, send_sem=sem, recv_sem=sem, device_id=SB, device_id_type=MESH)
+        if received:
+            cp.wait_recv()
+        else:
+            cp.wait_send()
+
     gp, gm, go = (g + 1) % 4, (g + 3) % 4, (g + 2) % 4
     xp, xm, xo = (x + 1) % 4, (x + 3) % 4, (x + 2) % 4
     yp, ym, yo = (y + 1) % 4, (y + 3) % 4, (y + 2) % 4
     XP, XM, YP, YM = dev(dx=1), dev(dx=3), dev(dy=1), dev(dy=3)
     ZP, ZM = dev(dz=1), dev(dz=3)
-    SB = dev(dc=1)
 
     def tile(i, yy, xx, first, count):
         return rall[i].at[yy // 2, yy % 2, xx // 2, xx % 2, c, pl.ds(first, count)]
@@ -95,7 +91,7 @@
         return rall[i].at[:, (y + 1) % 2, xh, xl, c, pl.ds(first, count)]
 
     def four(i, e, refs, to):
-        return [copy(GS, i, e + k, r, r, d) for k, (r, d) in enumerate(zip(refs, to))]
+        return [copy(gsend.at[i], grecv.at[i, e], r, r, d) for r, d in zip(refs, to)]
 
     def ag0(i):
         a, b = tile(i, y, x, 0, 256), tile(i, y, x, 256, 256)
@@ -111,23 +107,23 @@
 
     def ag2b(i):
         a, b = row(i, y, "near", 0, 256), col(i, x, "near", 256, 256)
-        return four(i, AG2 + 4, (a, a, b, b), (YP, YM, XP, XM))
+        return four(i, AG2, (a, a, b, b), (YP, YM, XP, XM))
 
     def ag2c(i):
         a, b = tile(i, y, xo, 0, 256), tile(i, yo, x, 256, 256)
-        return four(i, AG2 + 8, (a, a, b, b), (YP, YM, XP, XM))
+        return four(i, AG2C, (a, a, b, b), (YP, YM, XP, XM))
 
     def ag3a(i):
         return four(i, AG3, (tile(i, ym, x, 0, 128), tile(i, yp, x, 128, 128),
                              tile(i, y, xm, 256, 128), tile(i, y, xp, 384, 128)), (YP, YM, XP, XM))
 
     def ag3b(i):
-        return four(i, AG3 + 4, (row(i, ym, "near", 0, 128), row(i, yp, "near", 128, 128),
+        return four(i, AG3, (row(i, ym, "near", 0, 128), row(i, yp, "near", 128, 128),
                                  col(i, xm, "near", 256, 128), col(i, xp, "near", 384, 128)),
                     (YP, YM, XP, XM))
 
     def ag3c(i):
-        return four(i, AG3 + 8, (tile(i, ym, xo, 0, 128), tile(i, yp, xo, 128, 128),
+        return four(i, AG3, (tile(i, ym, xo, 0, 128), tile(i, yp, xo, 128, 128),
                                  tile(i, yo, xm, 256, 128), tile(i, yo, xp, 384, 128)),
                     (YP, YM, XP, XM))
 
@@ -136,51 +132,55 @@
                 rall[i].at[:, (y + 1) % 2, :, :, c, pl.ds(0, 256)],
                 rall[i].at[:, :, :, (x + 1) % 2, c, pl.ds(256, 256)],
                 row(i, yo, "all", 0, 256), col(i, xo, "all", 256, 256))
-        return [copy(GS, i, SIB + k, r, r, SB) for k, r in enumerate(refs)]
+        return [copy(gsend.at[i], grecv.at[i, SIB], r, r, SB) for r in refs]
 
     def g0(i):
         start(ag0(i) + ag2a(i))
 
     def g1(i):
-        arrive(ag0(i))
+        take(grecv.at[i, AG0], 256)
         start(ag1(i) + ag2b(i))
 
     def g2(i):
-        arrive(ag1(i))
+        take(grecv.at[i, AG1], 128)
         start(ag2c(i) + sib(i)[:2])
 
     def ga(i):
-        arrive(ag2a(i) + ag2b(i))
+        take(grecv.at[i, AG2], 768)
         start(ag3a(i) + ag3b(i))
 
     def g3(i):
-        arrive(ag2c(i))
+        take(grecv.at[i, AG2C], 256)
         start(ag3c(i) + sib(i)[2:4])
 
     def g4(i):
-        arrive(ag3a(i) + ag3b(i) + ag3c(i))
+        take(grecv.at[i, AG3], 512)
         start(sib(i)[4:])
 
-    def psi_copy(p):
-        return pltpu.make_async_copy(psi.at[p], inter.at[p], psem.at[p])
+    def psi_copy(k):
+        four_blocks = pl.ds(4 * k, 4)
+        return pltpu.make_async_copy(psi.at[four_blocks], inter.at[four_blocks], psem.at[k])
 
     def lp(i):
         @pl.loop(4 * i, 4 * i + 4)
         def _(p):
             inter[p] = jnp.dot(lmask[...], inter[p], preferred_element_type=F32).astype(BF16)
 
-    def passes(u, send_a, send_b, into, a, b):
-        return [copy(US, u, RS, send_a(go), into(0, a), ZM), copy(US, u, RS + 1, send_b(go), into(1, b), ZP),
-                copy(US, u, RS + 2, send_a(gp), into(2, a), ZP), copy(US, u, RS + 3, send_b(gm), into(3, b), ZM),
-                copy(US, u, RS + 4, send_a(gm), into(4, a), ZM), copy(US, u, RS + 5, send_b(gp), into(5, b), ZP)]
+    def passes(u, send_a, send_b, into):
+        def to(e, k, src, device):
+            return copy(rsend.at[u], urecv.at[u, e], src, into(k), device)
+
+        return [to(RS, 0, send_a(go), ZM), to(RSB, 1, send_b(go), ZP),
+                to(RSC, 2, send_a(gp), ZP), to(RSC, 3, send_b(gm), ZM),
+                to(RSC, 4, send_a(gm), ZM), to(RSC, 5, send_b(gp), ZP)]
 
     def rs(u):
         b, r = (u // 2) % 2, pl.ds((u % 2) * H, H)
         return passes(u, lambda d: part.at[b, d, pl.ds(0, HALF), r], lambda d: part.at[b, d, pl.ds(HALF, HALF), r],
-                      lambda k, _: rsin.at[u, k], 0, 1)
+                      lambda k: rsin.at[u, k])
 
     def rs0():
-        return passes(U, lambda d: part0.at[d, 0], lambda d: part0.at[d, 1], lambda k, _: rsin0.at[k], 0, 1)
+        return passes(U, lambda d: part0.at[d, 0], lambda d: part0.at[d, 1], lambda k: rsin0.at[k])
 
     def products(i, first):
         b = i % 2
@@ -196,7 +196,7 @@
                 part[b, d, j] = r[d * W:(d + 1) * W]
 
     def pr(i):
-        arrive(sib(i))
+        take(grecv.at[i, SIB], 2048)
         cs = rs(2 * i)
         products(i, 0)
         start([cs[0], cs[2]])
@@ -220,13 +220,12 @@
             cs[4 + k].start()
 
     def swap(u):
-        return copy(US, u, SWAP, w.at[u], v.at[u, c], SB)
+        return copy(xsend.at[u // 4], urecv.at[u, SWAP], w.at[u], v.at[u, c], SB)
 
     def fi(u):
         i, r = u // 2, slice((u % 2) * H, (u % 2) * H + H)
         b = i % 2
-        cs = rs(u)
-        arrive(cs[2:])
+        take(urecv.at[u, RSC], 448)
 
         @pl.loop(0, HALF, unroll=HALF)
         def _(j):
@@ -246,15 +245,14 @@
             v[u, c, ty, tx] = sigma[inv[(base + c) % 32]]
 
         swap(u).start()
-        sent(cs)
+        take(rsend.at[u], 672, False)
 
     def next_right():
-        return copy(US, U, SWAP, rmask, rnext, SB)
+        return copy(xsend.at[2], urecv.at[U, SWAP], rmask, rnext, SB)
 
     def s0(_):
-        @pl.loop(0, NP)
-        def _(p):
-            psi_copy(p).wait()
+        for k in range(4):
+            psi_copy(k).wait()
 
         cs = rs0()
         for k, ref in ((0, rmask), (1, rnext)):
@@ -276,8 +274,7 @@
             cs[4 + k].start()
 
     def s2(_):
-        cs = rs0()
-        arrive(cs[2:])
+        take(urecv.at[U, RSC], 512)
         for k in range(2):
             for i in range(C):
                 sigma0[k, i] = (part0[g, k, i].astype(F32) + rsin0[2 + k, i].astype(F32)
@@ -287,16 +284,16 @@
         cs = []
         for d in (1, 3, 2):
             tx, ty = (x + d) % 4, (y + d) % 4
-            cs.append(copy(US, u, A1 + d - 1, v.at[u, :, :, tx, pl.ds(0, Q)], x0.at[u, x], dev(dx=d)))
-            cs.append(copy(US, u, A1 + d + 2, v.at[u, :, ty, :, pl.ds(Q, Q)], x1.at[u, y], dev(dy=d)))
+            cs.append(copy(xsend.at[u // 4], urecv.at[u, A1], v.at[u, :, :, tx, pl.ds(0, Q)], x0.at[u, x], dev(dx=d)))
+            cs.append(copy(xsend.at[u // 4], urecv.at[u, A1], v.at[u, :, ty, :, pl.ds(Q, Q)], x1.at[u, y], dev(dy=d)))
         return cs
 
     def a2(u):
         cs = []
         for d in (1, 3, 2):
             tx, ty = (x + d) % 4, (y + d) % 4
-            cs.append(copy(US, u, A2 + d - 1, x0.at[u, :, :, ty], yf[u].at[y, :, :, pl.ds(0, Q)], dev(dy=d)))
-            cs.append(copy(US, u, A2 + d + 2, x1.at[u, :, :, tx], yf[u].at[:, x, :, pl.ds(Q, Q)], dev(dx=d)))
+            cs.append(copy(xsend.at[u // 4], urecv.at[u, A2], x0.at[u, :, :, ty], yf[u].at[y, :, :, pl.ds(0, Q)], dev(dy=d)))
+            cs.append(copy(xsend.at[u // 4], urecv.at[u, A2], x1.at[u, :, :, tx], yf[u].at[:, x, :, pl.ds(Q, Q)], dev(dx=d)))
         return cs
 
     def e1(u):
@@ -308,7 +305,7 @@
                 x1[u, y, q, k] = v[u, q, y, k, pl.ds(Q, Q)]
 
     def e2(u):
-        arrive(a1(u))
+        take(urecv.at[u, A1], 384)
         start(a2(u))
         for k in range(4):
             for q in range(2):
@@ -319,13 +316,13 @@
         return out.at[:, pl.ds(pl.multiple_of(g * W + (u % 2) * H, H), H), pl.ds((u // 2) * W, W)]
 
     def zout(u):
-        return [copy(US, u, ZOUT + d - 1, zbuf.at[u, (g + d) % 4], place(u), dev(dz=d)) for d in (2, 1, 3)]
+        return [copy(xsend.at[u // 4], urecv.at[u, ZOUT], zbuf.at[u, (g + d) % 4], place(u), dev(dz=d)) for d in (2, 1, 3)]
 
     def own_out(u):
         return pltpu.make_async_copy(zbuf.at[u, g], place(u), osem.at[u])
 
     def e3(u):
-        arrive(a2(u))
+        take(urecv.at[u, A2], 384)
 
         @pl.loop(0, NP, unroll=4)
         def _(p):
@@ -350,9 +347,8 @@
         right_copy(i).start()
     left_copy.start()
 
-    @pl.loop(0, NP)
-    def _(p):
-        psi_copy(p).start()
+    for k in range(4):
+        psi_copy(k).start()
 
     own = dims[s]
     rows = lax.broadcasted_iota(jnp.int32, (M, W), 0)
@@ -413,14 +409,14 @@
         step(i)
 
     for u in range(U):
-        arrive(zout(u))
+        take(urecv.at[u, ZOUT], 192)
         own_out(u).wait()
-
     for i in range(C):
-        sent(ag0(i) + ag1(i) + ag2a(i) + ag2b(i) + ag2c(i) + ag3a(i) + ag3b(i) + ag3c(i) + sib(i))
-    for u in range(U):
-        sent([swap(u)] + a1(u) + a2(u) + zout(u))
-    sent([next_right()] + rs0())
+        take(gsend.at[i], 3968, False)
+    for k in range(2):
+        take(xsend.at[k], 4864, False)
+    take(xsend.at[2], 512, False)
+    take(rsend.at[U], 768, False)
 
 
 def body(psi_blocks, left_env, right_env, shifts, sector_dims):
@@ -451,12 +447,13 @@
             pltpu.VMEM((U, 4, 4, H, W), BF16),
             pltpu.SMEM((32,), jnp.int32),
             pltpu.SMEM((4,), jnp.int32),
-            pltpu.SemaphoreType.DMA((NP,)),
+            pltpu.SemaphoreType.DMA((4,)),
             pltpu.SemaphoreType.DMA((C + 1,)),
             pltpu.SemaphoreType.DMA((U,)),
+            pltpu.SemaphoreType.DMA((C,)),
             pltpu.SemaphoreType.DMA((C, GATHER)),
-            pltpu.SemaphoreType.DMA((C, GATHER)),
-            pltpu.SemaphoreType.DMA((U + 1, UNIT)),
+            pltpu.SemaphoreType.DMA((U + 1,)),
+            pltpu.SemaphoreType.DMA((3,)),
             pltpu.SemaphoreType.DMA((U + 1, UNIT)),
             *[pltpu.VMEM((2, 2, 2, 2, 2, M, W), BF16)] * C,
             *[pltpu.VMEM((4, 4, 2, H, W), BF16)] * U,

time: 123 us -> 117 us (0.951)
  Pallas kernels: 119 us -> 114 us
    pallas_call x1, Pallas kernels: 119 us -> 114 us  [body(): pl.pallas_call(kernel, name='sigma', out_shape=jax.ShapeDtypeStruct((4, M...]
where the time goes in v4:
time: 117 us
  Pallas kernels  114 us (97%)
  local copies, waits for them, and re-layouts  3.05 us (3%)
    pallas_call x1, Pallas kernels, body(): pl.pallas_call(kernel, name='sigma', out_shape=jax.ShapeDtypeStruct((4, M...  114 us
    unnamed x1, local copies, waits for them, and re-layouts  3.05 us

profile of v4, /device:TPU:1, one launch (start us, length us, event | category | flops | bytes accessed | tf_op | source)
XLA Modules:
  0.0 116.6 jit_solution(14201515711954640784)
XLA Ops:
  0.0 113.5 %sigma.1 = bf16[4,512,512]{2,1,0:T(8,128)(2,1)} custom-call(s32[16]{0:T(128)} %shifts.1, s32[32]{0:T(128)} %dims.1, bf16[16,512,512]{2,1,0:T(8,128)(2,1)} %bitcast.5, bf16[512,512]{1,0:T(8,128)(2,1)} %bitcast.6, bf16[512,512]{1,0:T(8,128)(2,1)} %bitcast.7), custom_call_target="tpu_custom_call" | custom-call | flops 8589934592 | bytes 12582912 | tf_op jit(solution)/shard_map/sigma/pallas_call | solution.py:425
  113.5 3.0 %copy.7 = bf16[1,4,512,512]{3,2,1,0:T(8,128)(2,1)} copy(bf16[1,4,512,512]{3,2,1,0:T(8,128)(2,1)} %bitcast.4) | data formatting | bytes 4194304

commit v5 on v4

--- a/solution.py
+++ b/solution.py
@@ -425,9 +425,9 @@
     out = pl.pallas_call(
         kernel,
         name="sigma",
-        out_shape=jax.ShapeDtypeStruct((4, M, M), BF16),
+        out_shape=pltpu.VMEM((4, M, M), BF16),
         in_specs=[smem, smem, hbm, hbm, hbm],
-        out_specs=hbm,
+        out_specs=pl.BlockSpec(memory_space=pltpu.VMEM),
         scratch_shapes=[
             pltpu.VMEM((NP, M, M), BF16),
             pltpu.VMEM((M, M), BF16),

time: 117 us -> 115 us (0.983)
  local copies, waits for them, and re-layouts: 3.05 us -> 1.32 us
    unnamed x1, local copies, waits for them, and re-layouts: 3.05 us -> 1.32 us
where the time goes in v5:
time: 115 us
  Pallas kernels  114 us (99%)
  local copies, waits for them, and re-layouts  1.32 us (1%)
    pallas_call x1, Pallas kernels, body(): pl.pallas_call(kernel, name='sigma', out_shape=pltpu.VMEM((4, M, M), BF16...  114 us

profile of v5, /device:TPU:1, one launch (start us, length us, event | category | flops | bytes accessed | tf_op | source)
XLA Modules:
  0.0 114.9 jit_solution(4533861959305198834)
XLA Ops:
  0.0 113.5 %sigma.1 = bf16[4,512,512]{2,1,0:T(8,128)(2,1)S(1)} custom-call(s32[16]{0:T(128)} %shifts.1, s32[32]{0:T(128)} %dims.1, bf16[16,512,512]{2,1,0:T(8,128)(2,1)} %bitcast.5, bf16[512,512]{1,0:T(8,128)(2,1)} %bitcast.6, bf16[512,512]{1,0:T(8,128)(2,1)} %bitcast.7), custom_call_target="tpu_custom_call" | custom-call | flops 8589934592 | bytes 12582912 | tf_op jit(solution)/shard_map/sigma/pallas_call | solution.py:425
  113.5 1.3 %copy.7 = bf16[1,4,512,512]{3,2,1,0:T(8,128)(2,1)} copy(bf16[1,4,512,512]{3,2,1,0:T(8,128)(2,1)S(1)} %bitcast.4) | data formatting | bytes 4194304

commit v6 on v5

--- a/solution.py
+++ b/solution.py
@@ -395,15 +395,15 @@
         inv[k] = jnp.where(p == pb, jnp.int32(NR + 1), r)
 
     order = (
-        (g1, 0), (s0, 0), (g2, 0), (lp, 1), (ga, 0), (lp, 3), (g3, 0), (g0, 1), (s1, 0),
-        (lp, 2), (g4, 0), (g1, 1), (lp, 0), (g0, 3), (pr, 0), (s2, 0), (g2, 1), (g0, 2),
-        (ga, 1), (ps, 0), (g3, 1), (ad, 0), (g1, 2), (g4, 1), (g2, 2), (ad, 1), (g1, 3),
-        (pr, 1), (fi, 0), (ps, 1), (ga, 2), (g3, 2), (g2, 3), (ad, 2), (ga, 3), (g4, 2),
-        (e1, 0), (fi, 1), (g3, 3), (ad, 3), (pr, 2), (ps, 2), (fi, 2), (e1, 1), (g4, 3),
-        (e2, 0), (fi, 3), (e2, 1), (ad, 4), (pr, 3), (e1, 3), (e1, 2), (ad, 5), (fi, 4),
-        (e1, 4), (ps, 3), (e2, 3), (fi, 5), (ad, 6), (e3, 0), (e2, 4), (e1, 5), (ad, 7),
-        (e2, 2), (e3, 3), (e2, 5), (fi, 6), (e1, 6), (e3, 1), (fi, 7), (e1, 7), (e3, 5),
-        (e3, 4), (e3, 2), (e2, 6), (e2, 7), (e3, 6), (e3, 7),
+        (s0, 0), (g1, 0), (lp, 0), (g2, 0), (lp, 1), (ga, 0), (lp, 2), (g3, 0), (g0, 1),
+        (s1, 0), (lp, 3), (g4, 0), (g0, 2), (g1, 1), (pr, 0), (g2, 1), (ps, 0), (ga, 1),
+        (g3, 1), (ad, 0), (g1, 2), (g4, 1), (s2, 0), (g0, 3), (g2, 2), (ad, 1), (pr, 1),
+        (g1, 3), (ga, 2), (ps, 1), (fi, 0), (g3, 2), (g2, 3), (ga, 3), (fi, 1), (e1, 0),
+        (ad, 2), (g4, 2), (ad, 3), (pr, 2), (fi, 2), (g3, 3), (e1, 1), (e1, 2), (fi, 3),
+        (ps, 2), (g4, 3), (e2, 1), (ad, 4), (e1, 3), (e2, 2), (ad, 5), (pr, 3), (fi, 4),
+        (ps, 3), (fi, 5), (e1, 4), (e1, 5), (e2, 0), (ad, 6), (ad, 7), (e2, 3), (e3, 2),
+        (e2, 5), (fi, 6), (e3, 1), (e3, 0), (e1, 6), (fi, 7), (e2, 4), (e1, 7), (e2, 6),
+        (e3, 3), (e3, 4), (e2, 7), (e3, 5), (e3, 6), (e3, 7),
     )
     for step, i in order:
         step(i)

time: 115 us -> 114 us (level)
  no operation moved by 1% of the time
where the time goes in v6:
time: 114 us
  Pallas kernels  113 us (99%)
  local copies, waits for them, and re-layouts  1.32 us (1%)
    pallas_call x1, Pallas kernels, body(): pl.pallas_call(kernel, name='sigma', out_shape=pltpu.VMEM((4, M, M), BF16...  113 us

profile of v6, /device:TPU:1, one launch (start us, length us, event | category | flops | bytes accessed | tf_op | source)
XLA Modules:
  0.0 113.9 jit_solution(1825158406748499508)
XLA Ops:
  0.0 112.6 %sigma.1 = bf16[4,512,512]{2,1,0:T(8,128)(2,1)S(1)} custom-call(s32[16]{0:T(128)} %shifts.1, s32[32]{0:T(128)} %dims.1, bf16[16,512,512]{2,1,0:T(8,128)(2,1)} %bitcast.5, bf16[512,512]{1,0:T(8,128)(2,1)} %bitcast.6, bf16[512,512]{1,0:T(8,128)(2,1)} %bitcast.7), custom_call_target="tpu_custom_call" | custom-call | flops 8589934592 | bytes 12582912 | tf_op jit(solution)/shard_map/sigma/pallas_call | solution.py:425
  112.6 1.3 %copy.7 = bf16[1,4,512,512]{3,2,1,0:T(8,128)(2,1)} copy(bf16[1,4,512,512]{3,2,1,0:T(8,128)(2,1)S(1)} %bitcast.4) | data formatting | bytes 4194304

commit v7 on v6

--- a/solution.py
+++ b/solution.py
@@ -19,8 +19,8 @@
 NR = NP - 2
 HALF = NR // 2
 
-AG0, AG1, AG2, AG2C, AG3, SIB = range(6)
-GATHER = 6
+AG0, AG1, AG2, AG2C, AG3, AG3C, SIB = range(7)
+GATHER = 7
 RS, RSB, RSC, SWAP, A1, A2, ZOUT = range(7)
 UNIT = 7
 
@@ -123,16 +123,12 @@
                     (YP, YM, XP, XM))
 
     def ag3c(i):
-        return four(i, AG3, (tile(i, ym, xo, 0, 128), tile(i, yp, xo, 128, 128),
+        return four(i, AG3C, (tile(i, ym, xo, 0, 128), tile(i, yp, xo, 128, 128),
                                  tile(i, yo, xm, 256, 128), tile(i, yo, xp, 384, 128)),
                     (YP, YM, XP, XM))
 
-    def sib(i):
-        refs = (row(i, y, "all", 0, 256), col(i, x, "all", 256, 256),
-                rall[i].at[:, (y + 1) % 2, :, :, c, pl.ds(0, 256)],
-                rall[i].at[:, :, :, (x + 1) % 2, c, pl.ds(256, 256)],
-                row(i, yo, "all", 0, 256), col(i, xo, "all", 256, 256))
-        return [copy(gsend.at[i], grecv.at[i, SIB], r, r, SB) for r in refs]
+    def sib(i, *refs):
+        start([copy(gsend.at[i], grecv.at[i, SIB], r, r, SB) for r in refs])
 
     def g0(i):
         start(ag0(i) + ag2a(i))
@@ -143,26 +139,37 @@
 
     def g2(i):
         take(grecv.at[i, AG1], 128)
-        start(ag2c(i) + sib(i)[:2])
+        start(ag2c(i))
+        sib(i, row(i, y, "all", 0, 256), col(i, x, "all", 256, 256))
 
     def ga(i):
         take(grecv.at[i, AG2], 768)
         start(ag3a(i) + ag3b(i))
+        sib(i, rall[i].at[:, (y + 1) % 2, x // 2, x % 2, c, pl.ds(0, 256)],
+            rall[i].at[y // 2, y % 2, :, (x + 1) % 2, c, pl.ds(256, 256)],
+            rall[i].at[:, (y + 1) % 2, :, (x + 1) % 2, c])
 
     def g3(i):
         take(grecv.at[i, AG2C], 256)
-        start(ag3c(i) + sib(i)[2:4])
+        start(ag3c(i))
+        sib(i, rall[i].at[:, (y + 1) % 2, xo // 2, xo % 2, c, pl.ds(0, 256)],
+            rall[i].at[yo // 2, yo % 2, :, (x + 1) % 2, c, pl.ds(256, 256)])
+
+    def gb(i):
+        take(grecv.at[i, AG3], 384)
+        sib(i, tile(i, yo, x, 0, 256), row(i, yo, "near", 0, 256),
+            tile(i, y, xo, 256, 256), col(i, xo, "near", 256, 256))
 
     def g4(i):
-        take(grecv.at[i, AG3], 512)
-        start(sib(i)[4:])
+        take(grecv.at[i, AG3C], 128)
+        sib(i, tile(i, yo, xo, 0, 512))
 
     def psi_copy(k):
         four_blocks = pl.ds(4 * k, 4)
         return pltpu.make_async_copy(psi.at[four_blocks], inter.at[four_blocks], psem.at[k])
 
     def lp(i):
-        @pl.loop(4 * i, 4 * i + 4)
+        @pl.loop(4 * i, 4 * i + 4, unroll=2)
         def _(p):
             inter[p] = jnp.dot(lmask[...], inter[p], preferred_element_type=F32).astype(BF16)
 
@@ -175,8 +182,8 @@
                 to(RSC, 4, send_a(gm), ZM), to(RSC, 5, send_b(gp), ZP)]
 
     def rs(u):
-        b, r = (u // 2) % 2, pl.ds((u % 2) * H, H)
-        return passes(u, lambda d: part.at[b, d, pl.ds(0, HALF), r], lambda d: part.at[b, d, pl.ds(HALF, HALF), r],
+        b, h = (u // 2) % 2, u % 2
+        return passes(u, lambda d: part.at[b, d, h, pl.ds(0, HALF)], lambda d: part.at[b, d, h, pl.ds(HALF, HALF)],
                       lambda k: rsin.at[u, k])
 
     def rs0():
@@ -193,7 +200,8 @@
             r = jnp.dot(inter[p], rall[i][t // 16, (t // 8) % 2, (t // 4) % 2, (t // 2) % 2, t % 2],
                         preferred_element_type=F32).astype(BF16)
             for d in range(4):
-                part[b, d, j] = r[d * W:(d + 1) * W]
+                for h in range(2):
+                    part[b, d, h, j] = r[d * W + h * H:d * W + (h + 1) * H]
 
     def pr(i):
         take(grecv.at[i, SIB], 2048)
@@ -207,14 +215,14 @@
         start(rs(2 * i + 1)[:4])
 
     def ad(u):
-        b, r = (u // 2) % 2, slice((u % 2) * H, (u % 2) * H + H)
+        b, h = (u // 2) % 2, u % 2
         cs = rs(u)
         for k, d, first in ((0, gm, 0), (1, gp, HALF)):
             cs[k].wait_recv()
 
             @pl.loop(0, HALF, unroll=HALF)
             def _(j):
-                part[b, d, first + j, r] = (part[b, d, first + j, r].astype(F32)
+                part[b, d, h, first + j] = (part[b, d, h, first + j].astype(F32)
                                             + rsin[u, k, j].astype(F32)).astype(BF16)
 
             cs[4 + k].start()
@@ -224,14 +232,14 @@
 
     def fi(u):
         i, r = u // 2, slice((u % 2) * H, (u % 2) * H + H)
-        b = i % 2
+        b, h = i % 2, u % 2
         take(urecv.at[u, RSC], 448)
 
         @pl.loop(0, HALF, unroll=HALF)
         def _(j):
-            sigma[j] = (part[b, g, j, r].astype(F32) + rsin[u, 2, j].astype(F32)
+            sigma[j] = (part[b, g, h, j].astype(F32) + rsin[u, 2, j].astype(F32)
                         + rsin[u, 4, j].astype(F32)).astype(BF16)
-            sigma[j + HALF] = (part[b, g, j + HALF, r].astype(F32) + rsin[u, 3, j].astype(F32)
+            sigma[j + HALF] = (part[b, g, h, j + HALF].astype(F32) + rsin[u, 3, j].astype(F32)
                                + rsin[u, 5, j].astype(F32)).astype(BF16)
 
         sigma[NR] = sigma0[0, i, r]
@@ -387,23 +395,25 @@
     place_of[2] = pa
     place_of[3] = pb
 
-    @pl.loop(0, 32)
-    def _(k):
-        p = slot_of(k)
-        r = p - (p > low).astype(jnp.int32) - (p > high).astype(jnp.int32)
-        r = jnp.where(p == pa, jnp.int32(NR), r)
-        inv[k] = jnp.where(p == pb, jnp.int32(NR + 1), r)
+    def tb(_):
+        @pl.loop(0, 32)
+        def _(k):
+            p = slot_of(k)
+            r = p - (p > low).astype(jnp.int32) - (p > high).astype(jnp.int32)
+            r = jnp.where(p == pa, jnp.int32(NR), r)
+            inv[k] = jnp.where(p == pb, jnp.int32(NR + 1), r)
 
     order = (
         (s0, 0), (g1, 0), (lp, 0), (g2, 0), (lp, 1), (ga, 0), (lp, 2), (g3, 0), (g0, 1),
-        (s1, 0), (lp, 3), (g4, 0), (g0, 2), (g1, 1), (pr, 0), (g2, 1), (ps, 0), (ga, 1),
-        (g3, 1), (ad, 0), (g1, 2), (g4, 1), (s2, 0), (g0, 3), (g2, 2), (ad, 1), (pr, 1),
-        (g1, 3), (ga, 2), (ps, 1), (fi, 0), (g3, 2), (g2, 3), (ga, 3), (fi, 1), (e1, 0),
-        (ad, 2), (g4, 2), (ad, 3), (pr, 2), (fi, 2), (g3, 3), (e1, 1), (e1, 2), (fi, 3),
-        (ps, 2), (g4, 3), (e2, 1), (ad, 4), (e1, 3), (e2, 2), (ad, 5), (pr, 3), (fi, 4),
-        (ps, 3), (fi, 5), (e1, 4), (e1, 5), (e2, 0), (ad, 6), (ad, 7), (e2, 3), (e3, 2),
-        (e2, 5), (fi, 6), (e3, 1), (e3, 0), (e1, 6), (fi, 7), (e2, 4), (e1, 7), (e2, 6),
-        (e3, 3), (e3, 4), (e2, 7), (e3, 5), (e3, 6), (e3, 7),
+        (s1, 0), (lp, 3), (gb, 0), (g4, 0), (g0, 2), (g1, 1), (pr, 0), (tb, 0), (g2, 1), (ps, 0),
+        (ga, 1), (g3, 1), (ad, 0), (g1, 2), (gb, 1), (g4, 1), (s2, 0), (g0, 3), (g2, 2),
+        (ad, 1), (pr, 1), (g1, 3), (ga, 2), (ps, 1), (fi, 0), (g3, 2), (g2, 3), (ga, 3),
+        (fi, 1), (e1, 0), (ad, 2), (gb, 2), (g4, 2), (ad, 3), (pr, 2), (fi, 2), (g3, 3),
+        (e1, 1), (e1, 2), (fi, 3), (ps, 2), (gb, 3), (g4, 3), (e2, 1), (ad, 4), (e1, 3),
+        (e2, 2), (ad, 5), (pr, 3), (fi, 4), (ps, 3), (fi, 5), (e1, 4), (e1, 5), (e2, 0),
+        (ad, 6), (ad, 7), (e2, 3), (e3, 2), (e2, 5), (fi, 6), (e3, 1), (e3, 0), (e1, 6),
+        (fi, 7), (e2, 4), (e1, 7), (e2, 6), (e3, 3), (e3, 4), (e2, 7), (e3, 5), (e3, 6),
+        (e3, 7),
     )
     for step, i in order:
         step(i)
@@ -434,7 +444,7 @@
             pltpu.VMEM((M, M), BF16),
             pltpu.VMEM((M, M), BF16),
             pltpu.VMEM((M, M), BF16),
-            pltpu.VMEM((2, 4, NR, W, W), BF16),
+            pltpu.VMEM((2, 4, 2, NR, H, W), BF16),
             pltpu.VMEM((4, 2, C, W, W), BF16),
             pltpu.VMEM((U, 6, HALF, H, W), BF16),
             pltpu.VMEM((6, C, W, W), BF16),

time: 114 us -> 113 us (level)
  no operation moved by 1% of the time
where the time goes in v7:
time: 113 us
  Pallas kernels  112 us (99%)
  local copies, waits for them, and re-layouts  1.32 us (1%)
    pallas_call x1, Pallas kernels, body(): pl.pallas_call(kernel, name='sigma', out_shape=pltpu.VMEM((4, M, M), BF16...  112 us

profile of v7, /device:TPU:1, one launch (start us, length us, event | category | flops | bytes accessed | tf_op | source)
XLA Modules:
  0.0 113.3 jit_solution(18269581053173075297)
XLA Ops:
  0.0 111.9 %sigma.1 = bf16[4,512,512]{2,1,0:T(8,128)(2,1)S(1)} custom-call(s32[16]{0:T(128)} %shifts.1, s32[32]{0:T(128)} %dims.1, bf16[16,512,512]{2,1,0:T(8,128)(2,1)} %bitcast.5, bf16[512,512]{1,0:T(8,128)(2,1)} %bitcast.6, bf16[512,512]{1,0:T(8,128)(2,1)} %bitcast.7), custom_call_target="tpu_custom_call" | custom-call | flops 8589934592 | bytes 12582912 | tf_op jit(solution)/shard_map/sigma/pallas_call | solution.py:435
  111.9 1.3 %copy.7 = bf16[1,4,512,512]{3,2,1,0:T(8,128)(2,1)} copy(bf16[1,4,512,512]{3,2,1,0:T(8,128)(2,1)S(1)} %bitcast.4) | data formatting | bytes 4194304

commit v8 on v7

--- a/solution.py
+++ b/solution.py
@@ -42,7 +42,7 @@
 
 
 def kernel(shifts, dims, psi, left, right, out,
-           inter, early, lmask, rmask, rnext, part, part0, rsin, rsin0, sigma, sigma0,
+           inter, lmask, rmask, rnext, part, part0, rsin, rsin0, sigma, sigma0,
            v, w, x0, x1, zbuf, inv, place_of,
            psem, lsem, osem, gsend, grecv, rsend, xsend, urecv, *chunked):
     rall, yf = chunked[:C], chunked[C:]
@@ -169,6 +169,8 @@
         return pltpu.make_async_copy(psi.at[four_blocks], inter.at[four_blocks], psem.at[k])
 
     def lp(i):
+        psi_copy(i).wait()
+
         @pl.loop(4 * i, 4 * i + 4, unroll=2)
         def _(p):
             inter[p] = jnp.dot(lmask[...], inter[p], preferred_element_type=F32).astype(BF16)
@@ -259,15 +261,11 @@
         return copy(xsend.at[2], urecv.at[U, SWAP], rmask, rnext, SB)
 
     def s0(_):
-        for k in range(4):
-            psi_copy(k).wait()
-
         cs = rs0()
         for k, ref in ((0, rmask), (1, rnext)):
             if k:
                 next_right().wait_recv()
-            early[...] = jnp.dot(lmask[...], inter[place_of[2 + k]], preferred_element_type=F32).astype(BF16)
-            r = jnp.dot(early[...], ref[...], preferred_element_type=F32).astype(BF16)
+            r = jnp.dot(inter[place_of[2 + k]], ref[...], preferred_element_type=F32).astype(BF16)
             for d in range(4):
                 for i in range(C):
                     part0[d, k, i] = r[d * W:(d + 1) * W, i * W:(i + 1) * W]
@@ -404,16 +402,16 @@
             inv[k] = jnp.where(p == pb, jnp.int32(NR + 1), r)
 
     order = (
-        (s0, 0), (g1, 0), (lp, 0), (g2, 0), (lp, 1), (ga, 0), (lp, 2), (g3, 0), (g0, 1),
-        (s1, 0), (lp, 3), (gb, 0), (g4, 0), (g0, 2), (g1, 1), (pr, 0), (tb, 0), (g2, 1), (ps, 0),
-        (ga, 1), (g3, 1), (ad, 0), (g1, 2), (gb, 1), (g4, 1), (s2, 0), (g0, 3), (g2, 2),
-        (ad, 1), (pr, 1), (g1, 3), (ga, 2), (ps, 1), (fi, 0), (g3, 2), (g2, 3), (ga, 3),
-        (fi, 1), (e1, 0), (ad, 2), (gb, 2), (g4, 2), (ad, 3), (pr, 2), (fi, 2), (g3, 3),
-        (e1, 1), (e1, 2), (fi, 3), (ps, 2), (gb, 3), (g4, 3), (e2, 1), (ad, 4), (e1, 3),
-        (e2, 2), (ad, 5), (pr, 3), (fi, 4), (ps, 3), (fi, 5), (e1, 4), (e1, 5), (e2, 0),
-        (ad, 6), (ad, 7), (e2, 3), (e3, 2), (e2, 5), (fi, 6), (e3, 1), (e3, 0), (e1, 6),
-        (fi, 7), (e2, 4), (e1, 7), (e2, 6), (e3, 3), (e3, 4), (e2, 7), (e3, 5), (e3, 6),
-        (e3, 7),
+        (g1, 0), (lp, 0), (lp, 1), (g2, 0), (lp, 2), (ga, 0), (lp, 3), (s0, 0), (g3, 0),
+        (g0, 1), (gb, 0), (g4, 0), (s1, 0), (g0, 2), (g1, 1), (pr, 0), (tb, 0), (g2, 1),
+        (ps, 0), (ga, 1), (g3, 1), (ad, 0), (g1, 2), (gb, 1), (g4, 1), (s2, 0), (g0, 3),
+        (g2, 2), (ad, 1), (pr, 1), (g1, 3), (ga, 2), (ps, 1), (fi, 0), (g3, 2), (g2, 3),
+        (ga, 3), (fi, 1), (e1, 0), (ad, 2), (gb, 2), (g4, 2), (ad, 3), (pr, 2), (fi, 2),
+        (g3, 3), (e1, 1), (e1, 2), (fi, 3), (ps, 2), (gb, 3), (g4, 3), (e2, 1), (ad, 4),
+        (e1, 3), (e2, 2), (ad, 5), (pr, 3), (fi, 4), (ps, 3), (fi, 5), (e1, 4), (e1, 5),
+        (e2, 0), (ad, 6), (ad, 7), (e2, 3), (e3, 2), (e2, 5), (fi, 6), (e3, 1), (e3, 0),
+        (e1, 6), (fi, 7), (e2, 4), (e1, 7), (e2, 6), (e3, 3), (e3, 4), (e2, 7), (e3, 5),
+        (e3, 6), (e3, 7),
     )
     for step, i in order:
         step(i)
@@ -440,7 +438,6 @@
         out_specs=pl.BlockSpec(memory_space=pltpu.VMEM),
         scratch_shapes=[
             pltpu.VMEM((NP, M, M), BF16),
-            pltpu.VMEM((M, M), BF16),
             pltpu.VMEM((M, M), BF16),
             pltpu.VMEM((M, M), BF16),
             pltpu.VMEM((M, M), BF16),

time: 113 us -> 117 us (1.035)
  Pallas kernels: 112 us -> 115 us
    pallas_call x1, Pallas kernels: 112 us -> 115 us  [body(): pl.pallas_call(kernel, name='sigma', out_shape=pltpu.VMEM((4, M, M), BF16...]
where the time goes in v8:
time: 117 us
  Pallas kernels  115 us (98%)
  local copies, waits for them, and re-layouts  1.32 us (1%)
    pallas_call x1, Pallas kernels, body(): pl.pallas_call(kernel, name='sigma', out_shape=pltpu.VMEM((4, M, M), BF16...  115 us

profile of v8, /device:TPU:1, one launch (start us, length us, event | category | flops | bytes accessed | tf_op | source)
XLA Modules:
  0.0 116.5 jit_solution(10035832506841225893)
XLA Ops:
  0.0 115.2 %sigma.1 = bf16[4,512,512]{2,1,0:T(8,128)(2,1)S(1)} custom-call(s32[16]{0:T(128)} %shifts.1, s32[32]{0:T(128)} %dims.1, bf16[16,512,512]{2,1,0:T(8,128)(2,1)} %bitcast.5, bf16[512,512]{1,0:T(8,128)(2,1)} %bitcast.6, bf16[512,512]{1,0:T(8,128)(2,1)} %bitcast.7), custom_call_target="tpu_custom_call" | custom-call | flops 8589934592 | bytes 12582912 | tf_op jit(solution)/shard_map/sigma/pallas_call | solution.py:433
  115.2 1.3 %copy.7 = bf16[1,4,512,512]{3,2,1,0:T(8,128)(2,1)} copy(bf16[1,4,512,512]{3,2,1,0:T(8,128)(2,1)S(1)} %bitcast.4) | data formatting | bytes 4194304
